TPU v7x, 1024 devices: a whole 4x8x16 slice. The times are simulated.
1024 devices in a mesh: grp: 8 (over y), sub: 128 (over z, x, core).
Axes of the slice: x: 4, y: 8, z: 16, core: 2. Of those that a mesh axis runs over, the one named last changes fastest.
Arguments:
- rhs: float32 [8, 128, 8, 2048], P('grp', 'sub'), may hold values from -6 to 6
- diagonal: float32 [8, 128, 2048], P('grp', 'sub'), may hold values from 3 to 6
- blocks: float32 [8, 128, 32, 3, 64, 64], P('grp', 'sub'), may hold values from -0.4375 to 0.4375
- pattern: int32 [8, 128, 32, 3], P('grp', 'sub'), may hold values from 0 to 31
- margin: int32 [8, 128, 4, 4], P('grp', 'sub'), may hold values from 0 to 15
- basis: float32 [8, 128, 48, 2048], P('grp', 'sub'), may hold values from -0.25 to 0.25
- coarse_inverse: float32 [8, 6144, 6144], P('grp', 'sub'), as said below
Outputs:
- solution: float32 [8, 128, 8, 2048], P('grp', 'sub')
Inputs may be any that keep to these rules, and one draw needn't show every extreme that they name: `coarse_inverse`: each group's matrix is symmetric.
All inputs are finite; a program needn't handle non-finite values.
Results may differ from a plain program's by a relative error of at most 0.0003.
Values sent between devices are 32-bit elements; how exact they have to be, the bound alone decides.
No kernel may reach another device: no remote copies, remote signals or barrier semaphores. Data moves between devices by JAX's collectives and lax.ppermute only.
A program may use at most 32 MiB of HBM per device.

v0:
```python
import jax
import jax.numpy as jnp
from jax import lax
from jax.sharding import PartitionSpec as P

ITERS = 3


def extended(value, sides, width):
    for axis, dim in sides:
        size, length = (lax.axis_size(axis), value.shape[dim])
        up = [(i, (i + 1) % size) for i in range(size - 1)]
        down = [(j, i) for i, j in up]
        last = lax.slice_in_dim(value, length - width, length, axis=dim)
        first = lax.slice_in_dim(value, 0, width, axis=dim)
        before = lax.ppermute(last, axis, up)
        after = lax.ppermute(first, axis, down)
        value = jnp.concatenate([before, value, after], axis=dim)
    return value


def least_squares(columns, beta):
    ortho = []
    upper = []
    for k in range(len(columns)):
        vector = columns[k]
        coeffs = []
        for i in range(k):
            weight = jnp.sum(ortho[i] * columns[k], axis=-1)
            coeffs.append(weight)
            vector = vector - weight[:, None] * ortho[i]
        length = jnp.sqrt(jnp.sum(vector * vector, axis=-1))
        coeffs.append(length)
        upper.append(coeffs)
        ortho.append(vector / length[:, None])
    target = [ortho[k][:, 0] * beta for k in range(len(columns))]
    result = [None] * len(columns)
    for k in reversed(range(len(columns))):
        value = target[k]
        for i in range(k + 1, len(columns)):
            value = value - upper[i][k] * result[i]
        result[k] = value / upper[k][k]
    return result


def operate(field, blocks, pattern, diagonal, margin):
    count, rows = field.shape
    nblocks = pattern.shape[0]
    width = rows // nblocks
    picked = field.reshape(count, nblocks, width)[:, pattern]
    local = jnp.einsum("bkoi,nbki->nbo", blocks, picked, precision=lax.Precision.HIGHEST).reshape(
        count, rows
    )
    tiles = field.reshape(count, rows // 128, 128)
    send = tiles[:, margin].reshape(count, 4, -1)
    grp_in = extended(jnp.stack([send[:, 0], send[:, 1]]), (("grp", 0),), 1)
    sub_in = extended(jnp.stack([send[:, 2], send[:, 3]]), (("sub", 0),), 1)
    received = jnp.stack([grp_in[0], grp_in[3], sub_in[0], sub_in[3]], axis=1)
    zeros = jnp.zeros((count, rows // 128, 128), jnp.float32)
    coupled = zeros.at[:, margin.reshape(-1)].add(received.reshape(count, -1, 128))
    return diagonal[None, :] * field + local - coupled.reshape(count, rows)


def precondition(field, diagonal, basis, inverse_rows):
    coarse_part = lax.dot_general(
        field, basis, (((1,), (1,)), ((), ())), precision=lax.Precision.HIGHEST
    )
    answer = lax.dot_general(
        lax.all_gather(coarse_part, "sub", axis=1, tiled=True),
        inverse_rows,
        (((1,), (1,)), ((), ())),
        precision=lax.Precision.HIGHEST,
    )
    back = jnp.dot(answer, basis, precision=lax.Precision.HIGHEST)
    return field / diagonal[None, :] + back


def global_sums(values):
    return lax.psum(values, ("grp", "sub"))


def per_device(rhs, diagonal, blocks, pattern, margin, basis, coarse_inverse):
    source = rhs[0, 0]
    diag_row = diagonal[0, 0]
    local_blocks = blocks[0, 0]
    local_pattern = pattern[0, 0]
    local_margin = margin[0, 0]
    local_basis = basis[0, 0]
    inverse_rows = coarse_inverse[0]
    beta = jnp.sqrt(global_sums(jnp.sum(source * source, axis=-1)[None])[0])
    vectors = [source / beta[:, None]]
    columns = []
    conditioned = []
    for step in range(ITERS):
        pre = precondition(vectors[step], diag_row, local_basis, inverse_rows)
        pre, image = (pre, operate(pre, local_blocks, local_pattern, diag_row, local_margin))
        locals_list = [jnp.sum(vec * image, axis=-1) for vec in vectors] + [
            jnp.sum(image * image, axis=-1)
        ]
        sums = global_sums(jnp.stack(locals_list))
        dots = [sums[i] for i in range(step + 1)]
        square = sums[step + 1]
        conditioned.append(pre)
        rest = image
        heights = jnp.zeros_like(square)
        for i in range(step + 1):
            rest = rest - dots[i][:, None] * vectors[i]
            heights = heights + dots[i] * dots[i]
        height = jnp.sqrt(jnp.maximum(square - heights, 0.001 * square))
        entries = dots + [height] + [jnp.zeros_like(height)] * (ITERS - step - 1)
        columns.append(jnp.stack(entries, axis=-1))
        vectors.append(rest / height[:, None])
    coeffs = least_squares(columns, beta)
    combo = jnp.zeros_like(source)
    for i in range(ITERS):
        combo = combo + coeffs[i][:, None] * vectors[i]
    result = precondition(combo, diag_row, local_basis, inverse_rows)
    return result[None, None]


def solution(mesh):
    in_specs = (
        P("grp", "sub", None, None),
        P("grp", "sub", None),
        P("grp", "sub", None, None, None, None),
        P("grp", "sub", None, None),
        P("grp", "sub", None, None),
        P("grp", "sub", None, None),
        P("grp", "sub", None),
    )
    out_specs = P("grp", "sub", None, None)
    return jax.shard_map(
        per_device, mesh=mesh, in_specs=in_specs, out_specs=out_specs, check_vma=False
    )
```

profile of v0, /device:TPU:1, one launch (start us, length us, event | category | flops | bytes accessed | tf_op | source)
XLA Modules:
  0.0 992.3 jit_solution(13233650105096805721)
XLA Ops:
  1.1 136.9 %psum.28 = f32[1,8]{1,0:T(1,128)S(1)} all-reduce(f32[1,8]{1,0:T(1,128)S(1)} %bitcast.372), channel_id=1, replica_groups=mesh['grp'=8,'sub'=128] {'grp','sub'}, use_global_device_ids=true, to_apply=%region_1.0 | all-reduce | flops 8 | bytes 64 | tf_op jit(solution)/shard_map/psum | solution.py:79
  140.0 81.0 %all-gather = f32[128,48,8]{1,2,0:T(8,128)S(1)} all-gather(f32[1,48,8]{1,2,0:T(8,128)S(1)} %convolution_bitcast_fusion.3), channel_id=1, replica_groups=mesh['grp'=8,'sub'=128] {'sub'}, dimensions={0}, use_global_device_ids=true | all-gather | bytes 198144 | tf_op jit(solution)/shard_map/all_gather | solution.py:69
  222.0 2.0 reshape.457
  226.6 2.4 fusion.13
  229.9 2.0 gather_fusion.1
  236.5 2.9 collective-permute-start.2
  239.4 2.0 collective-permute-start.3
  249.3 2.3 gather_fusion
  251.5 4.4 fusion.15
  264.5 2.5 scatter_fusion
  269.9 120.0 %psum.29 = f32[2,8]{1,0:T(2,128)} all-reduce(f32[2,8]{1,0:T(2,128)} %pad_maximum_fusion.6), channel_id=1, replica_groups=mesh['grp'=8,'sub'=128] {'grp','sub'}, use_global_device_ids=true, to_apply=%region_5.0 | all-reduce | flops 16 | bytes 128 | tf_op jit(solution)/shard_map/psum | solution.py:79
  395.2 82.3 %all-gather.1 = f32[128,48,8]{1,2,0:T(8,128)S(1)} all-gather(f32[1,48,8]{1,2,0:T(8,128)S(1)} %convolution_bitcast_fusion.2), channel_id=1, replica_groups=mesh['grp'=8,'sub'=128] {'sub'}, dimensions={0}, use_global_device_ids=true | all-gather | bytes 198144 | tf_op jit(solution)/shard_map/all_gather | solution.py:69
  480.5 2.4 fusion.11
  487.1 2.3 gather_fusion.2
  489.3 5.1 fusion.18
  494.4 2.1 gather_fusion.3
  503.1 3.0 collective-permute-start.7
  515.6 2.4 scatter_fusion.1
  521.6 122.4 %psum.30 = f32[3,8]{1,0:T(4,128)} all-reduce(f32[3,8]{1,0:T(4,128)} %pad_maximum_fusion.3), channel_id=1, replica_groups=mesh['grp'=8,'sub'=128] {'grp','sub'}, use_global_device_ids=true, to_apply=%region_11.0 | all-reduce | flops 24 | bytes 192 | tf_op jit(solution)/shard_map/psum | solution.py:79
  649.6 80.4 %all-gather.2 = f32[128,48,8]{1,2,0:T(8,128)S(1)} all-gather(f32[1,48,8]{1,2,0:T(8,128)S(1)} %convolution_bitcast_fusion.1), channel_id=1, replica_groups=mesh['grp'=8,'sub'=128] {'sub'}, dimensions={0}, use_global_device_ids=true | all-gather | bytes 198144 | tf_op jit(solution)/shard_map/all_gather | solution.py:69
  732.8 2.4 fusion.9
  739.4 2.3 gather_fusion.4
  741.7 5.1 fusion.21
  746.8 2.0 gather_fusion.5
  750.2 3.5 collective-permute-start.8
  755.0 2.7 collective-permute-start.10
  757.7 2.2 collective-permute-start.11
  770.8 2.4 scatter_fusion.2
  776.2 123.9 %psum.31 = f32[4,8]{1,0:T(4,128)} all-reduce(f32[4,8]{1,0:T(4,128)} %pad_maximum_fusion.4), channel_id=1, replica_groups=mesh['grp'=8,'sub'=128] {'grp','sub'}, use_global_device_ids=true, to_apply=%region_19.0 | all-reduce | flops 32 | bytes 256 | tf_op jit(solution)/shard_map/psum | solution.py:79
  905.2 80.8 %all-gather.3 = f32[128,48,8]{1,2,0:T(8,128)S(1)} all-gather(f32[1,48,8]{1,2,0:T(8,128)S(1)} %convolution_bitcast_fusion), channel_id=1, replica_groups=mesh['grp'=8,'sub'=128] {'sub'}, dimensions={0}, use_global_device_ids=true | all-gather | bytes 198144 | tf_op jit(solution)/shard_map/all_gather | solution.py:69
  986.9 2.0 reshape.463
  988.9 2.4 fusion.7
  (164 shorter events, 99.3 us)
Async XLA Ops:
  0.0 251.5 %copy-start = (f32[1,1,32,3,64,64]{5,4,3,2,1,0:T(8,128)S(1)}, f32[1,1,32,3,64,64]{5,4,3,2,1,0:T(8,128)}, u32[]{:S(2)}) copy-start(f32[1,1,32,3,64,64]{5,4,3,2,1,0:T(8,128)} %param.9) | copy-start | bytes 4718596
  140.0 84.0 %copy-start.14 = (s32[1,1,4,4]{3,2,1,0:T(4,128)S(1)}, s32[1,1,4,4]{3,2,1,0:T(4,128)}, u32[]{:S(2)}) copy-start(s32[1,1,4,4]{3,2,1,0:T(4,128)} %param.11) | copy-start | bytes 196
  222.0 7.0 copy-start.1
  222.0 7.0 copy-start.11
  225.9 3.1 copy-start.2
  226.6 17.8 %copy-start.12 = (s32[1024]{0:T(1024)}, s32[1024]{0:T(1024)S(1)}, u32[]{:S(2)}) copy-start(s32[1024]{0:T(1024)S(1)} %pad_clamp_fusion) | copy-start | bytes 12292
  233.4 26.1 %collective-permute-start = (f32[1,8,512]{2,1,0:T(8,128)}, f32[1,8,512]{2,1,0:T(8,128)}, u32[]{:S(2)}, u32[]{:S(2)}) collective-permute-start(f32[1,8,512]{2,1,0:T(8,128)} %get-tuple-element.34), channel_id=1, source_target_pairs={{0,128},{128,256},{256,384},{384,512},{512,640},{640,768},{768,896... | collective-permute-start | bytes 49160 | tf_op jit(solution)/shard_map/ppermute | solution.py:16
  235.2 24.2 %collective-permute-start.1 = (f32[1,8,512]{2,1,0:T(8,128)}, f32[1,8,512]{2,1,0:T(8,128)}, u32[]{:S(2)}, u32[]{:S(2)}) collective-permute-start(f32[1,8,512]{2,1,0:T(8,128)} %get-tuple-element.37), channel_id=1, source_target_pairs={{128,0},{256,128},{384,256},{512,384},{640,512},{768,640},{896,768... | collective-permute-start | bytes 49160 | tf_op jit(solution)/shard_map/ppermute | solution.py:17
  236.5 22.9 %collective-permute-start.2 = (f32[1,8,512]{2,1,0:T(8,128)}, f32[1,8,512]{2,1,0:T(8,128)}, u32[]{:S(2)}, u32[]{:S(2)}) collective-permute-start(f32[1,8,512]{2,1,0:T(8,128)} %get-tuple-element.36), channel_id=1, source_target_pairs={{0,1},{1,2},{2,3},{3,4},{4,5},{5,6},{6,7},{7,8},{8,9},{9,10},{10,1... | collective-permute-start | bytes 49160 | tf_op jit(solution)/shard_map/ppermute | solution.py:16
  239.4 20.0 %collective-permute-start.3 = (f32[1,8,512]{2,1,0:T(8,128)}, f32[1,8,512]{2,1,0:T(8,128)}, u32[]{:S(2)}, u32[]{:S(2)}) collective-permute-start(f32[1,8,512]{2,1,0:T(8,128)} %get-tuple-element.35), channel_id=1, source_target_pairs={{1,0},{2,1},{3,2},{4,3},{5,4},{6,5},{7,6},{8,7},{9,8},{10,9},{11,1... | collective-permute-start | bytes 49160 | tf_op jit(solution)/shard_map/ppermute | solution.py:17
  251.5 4.5 copy-start.23
  391.9 3.3 copy-start.21
  480.5 2.5 copy-start.10
  480.5 2.5 copy-start.20
  480.5 2.5 copy-start.22
  498.0 12.6 %collective-permute-start.4 = (f32[1,8,512]{2,1,0:T(8,128)}, f32[1,8,512]{2,1,0:T(8,128)}, u32[]{:S(2)}, u32[]{:S(2)}) collective-permute-start(f32[1,8,512]{2,1,0:T(8,128)} %get-tuple-element.30), channel_id=1, source_target_pairs={{0,128},{128,256},{256,384},{384,512},{512,640},{640,768},{768,896... | collective-permute-start | bytes 49160 | tf_op jit(solution)/shard_map/ppermute | solution.py:16
  499.8 10.7 %collective-permute-start.5 = (f32[1,8,512]{2,1,0:T(8,128)}, f32[1,8,512]{2,1,0:T(8,128)}, u32[]{:S(2)}, u32[]{:S(2)}) collective-permute-start(f32[1,8,512]{2,1,0:T(8,128)} %get-tuple-element.33), channel_id=1, source_target_pairs={{128,0},{256,128},{384,256},{512,384},{640,512},{768,640},{896,768... | collective-permute-start | bytes 49160 | tf_op jit(solution)/shard_map/ppermute | solution.py:17
  501.1 9.4 collective-permute-start.6
  503.1 7.5 collective-permute-start.7
  732.8 2.4 copy-start.17
  741.7 5.1 copy-start.13
  750.2 15.6 %collective-permute-start.8 = (f32[1,8,512]{2,1,0:T(8,128)}, f32[1,8,512]{2,1,0:T(8,128)}, u32[]{:S(2)}, u32[]{:S(2)}) collective-permute-start(f32[1,8,512]{2,1,0:T(8,128)} %get-tuple-element.26), channel_id=1, source_target_pairs={{0,128},{128,256},{256,384},{384,512},{512,640},{640,768},{768,896... | collective-permute-start | bytes 49160 | tf_op jit(solution)/shard_map/ppermute | solution.py:16
  753.7 12.0 %collective-permute-start.9 = (f32[1,8,512]{2,1,0:T(8,128)}, f32[1,8,512]{2,1,0:T(8,128)}, u32[]{:S(2)}, u32[]{:S(2)}) collective-permute-start(f32[1,8,512]{2,1,0:T(8,128)} %get-tuple-element.29), channel_id=1, source_target_pairs={{128,0},{256,128},{384,256},{512,384},{640,512},{768,640},{896,768... | collective-permute-start | bytes 49160 | tf_op jit(solution)/shard_map/ppermute | solution.py:17
  755.0 10.8 %collective-permute-start.10 = (f32[1,8,512]{2,1,0:T(8,128)}, f32[1,8,512]{2,1,0:T(8,128)}, u32[]{:S(2)}, u32[]{:S(2)}) collective-permute-start(f32[1,8,512]{2,1,0:T(8,128)} %get-tuple-element.28), channel_id=1, source_target_pairs={{0,1},{1,2},{2,3},{3,4},{4,5},{5,6},{6,7},{7,8},{8,9},{9,10},{10,1... | collective-permute-start | bytes 49160 | tf_op jit(solution)/shard_map/ppermute | solution.py:16
  757.7 8.0 collective-permute-start.11
  986.9 4.4 copy-start.18
  988.8 2.5 copy-start.4
  988.9 2.5 copy-start.6
  988.9 2.5 copy-start.9
  988.9 2.5 copy-start.26
  988.9 2.5 copy-start.28
  988.9 2.5 copy-start.30
  (11 other events, 15.7 us)
where the time goes:
time: 1000 us; the launch traced here: 992 us
  blocking collectives  828 us (83%)
  local copies, waits for them, and re-layouts  74.2 us (7%)
  other arithmetic  32.3 us (3%)
  matrix products  31.8 us (3%)
  starting transfers between devices  25.8 us (3%)
    psum x4, blocking collectives, global_sums(): return lax.psum(values, ('grp', 'sub'))  503 us
    all_gather x4, blocking collectives, precondition(): lax.all_gather(coarse_part, 'sub', axis=1, tiled=True)  325 us
  transfers between devices with their start and end apart: 12, of which 0 were waited for; matrix products, arithmetic and copies ran while one was open for 3% of the time, Pallas kernels for 0%

commit v1 on v0

v1 whole, which is shorter than its diff:
```python
import jax
import jax.numpy as jnp
from jax import lax
from jax.sharding import Mesh, PartitionSpec as P

ITERS = 3
SUB = ("z", "x", "core")
HIGH = lax.Precision.HIGHEST


def gathered(value, axis):
    size = lax.axis_size(axis)
    return lax.all_to_all(jnp.broadcast_to(value[None], (size,) + value.shape), axis, 0, 0)


def gather_coarse(piece):
    count, width = piece.shape
    pair = lax.all_gather(piece, "core", axis=1, tiled=True)
    whole = gathered(gathered(pair, "z"), "x")
    return jnp.transpose(whole, (2, 1, 0, 3)).reshape(count, -1)


def total(values):
    values = jnp.sum(gathered(values, ("x", "core")), axis=0)
    values = jnp.sum(gathered(values, "z"), axis=0)
    return jnp.sum(gathered(values, "grp"), axis=0)


def least_squares(columns, beta):
    ortho = []
    upper = []
    for k in range(len(columns)):
        vector = columns[k]
        coeffs = []
        for i in range(k):
            weight = sum(a * b for a, b in zip(ortho[i], columns[k]))
            coeffs.append(weight)
            vector = [a - weight * b for a, b in zip(vector, ortho[i])]
        length = jnp.sqrt(sum(a * a for a in vector))
        coeffs.append(length)
        upper.append(coeffs)
        ortho.append([a / length for a in vector])
    result = [None] * len(columns)
    for k in reversed(range(len(columns))):
        value = ortho[k][0] * beta
        for i in range(k + 1, len(columns)):
            value = value - upper[i][k] * result[i]
        result[k] = value / upper[k][k]
    return result


def combine(gram):
    size = ITERS + 1
    full = [[gram[min(i, j)][max(i, j)] for j in range(size)] for i in range(size)]
    zero = jnp.zeros_like(full[0][0])

    def inner(a, b):
        return sum(
            a[i] * sum(full[i][j] * b[j] for j in range(size) if b[j] is not None)
            for i in range(size)
            if a[i] is not None
        )

    beta = jnp.sqrt(full[0][0])
    vectors = [[1.0 / beta] + [None] * ITERS]
    columns = []
    for step in range(ITERS):
        image = [None] + vectors[step][:ITERS]
        square = inner(image, image)
        dots = [inner(vec, image) for vec in vectors]
        heights = sum(d * d for d in dots)
        height = jnp.sqrt(jnp.maximum(square - heights, 0.001 * square))
        columns.append(dots + [height] + [zero] * (ITERS - step - 1))
        rest = []
        for m in range(size):
            terms = [(dots[i], vectors[i][m]) for i in range(step + 1) if vectors[i][m] is not None]
            if image[m] is None and not terms:
                rest.append(None)
                continue
            value = zero if image[m] is None else image[m]
            for dot, factor in terms:
                value = value - dot * factor
            rest.append(value / height)
        vectors.append(rest)
    weights = least_squares(columns, beta)
    return [
        sum(weights[i] * vectors[i][m] for i in range(ITERS) if vectors[i][m] is not None)
        for m in range(ITERS)
    ]


def local_part(field, blocks, pattern, diagonal):
    count, rows = field.shape
    nblocks = pattern.shape[0]
    picked = field.reshape(count, nblocks, rows // nblocks)[:, pattern]
    local = jnp.einsum("bkoi,nbki->nbo", blocks, picked, precision=HIGH).reshape(count, rows)
    return diagonal[None, :] * field + local


def exchange(field, margin, core):
    count, rows = field.shape
    rims = field.reshape(count, rows // 128, 128)[:, margin].reshape(count, 4, -1)
    groups = lax.axis_size("grp")
    subs = lax.axis_size(SUB)
    up = [(i, i + 1) for i in range(groups - 1)]
    down = [(j, i) for i, j in up]
    across = [(i, ((i + 1) ^ 1) - 1) for i in range(1, subs - 1)]
    from_low = lax.ppermute(rims[:, 1], "grp", up)
    from_high = lax.ppermute(rims[:, 0], "grp", down)
    first = core == 0
    other = lax.ppermute(jnp.where(first, rims[:, 2], rims[:, 3]), SUB, across)
    both = lax.all_gather(jnp.where(first, rims[:, 3], rims[:, 2]), "core")
    partner = jnp.where(first, both[1], both[0])
    sub_low = jnp.where(first, other, partner)
    sub_high = jnp.where(first, partner, other)
    received = jnp.stack([from_low, from_high, sub_low, sub_high], axis=1)
    zeros = jnp.zeros((count, rows // 128, 128), jnp.float32)
    coupled = zeros.at[:, margin.reshape(-1)].add(received.reshape(count, -1, 128))
    return coupled.reshape(count, rows)


def per_device(rhs, diagonal, blocks, pattern, margin, basis, coarse_inverse):
    source = rhs[0, 0]
    diag_row = diagonal[0, 0]
    local_blocks = blocks[0, 0]
    local_pattern = pattern[0, 0]
    local_margin = margin[0, 0]
    local_basis = basis[0, 0]
    inverse_rows = coarse_inverse[0]
    core = lax.axis_index("core")
    krylov = [source]
    conditioned = []
    for _ in range(ITERS):
        field = krylov[-1]
        piece = lax.dot_general(field, local_basis, (((1,), (1,)), ((), ())), precision=HIGH)
        answer = lax.dot_general(
            gather_coarse(piece), inverse_rows, (((1,), (1,)), ((), ())), precision=HIGH
        )
        pre = field / diag_row[None, :] + jnp.dot(answer, local_basis, precision=HIGH)
        conditioned.append(pre)
        base = local_part(pre, local_blocks, local_pattern, diag_row)
        krylov.append(base - exchange(pre, local_margin, core))
    pairs = [(i, j) for j in range(ITERS + 1) for i in range(j + 1)]
    sums = total(jnp.stack([jnp.sum(krylov[i] * krylov[j], axis=-1) for i, j in pairs]))
    gram = [[None] * (ITERS + 1) for _ in range(ITERS + 1)]
    for at, (i, j) in enumerate(pairs):
        gram[i][j] = sums[at]
    factors = combine(gram)
    result = sum(f[:, None] * p for f, p in zip(factors, conditioned))
    return result[None, None]


def solution(mesh):
    groups = mesh.shape["grp"]
    split = Mesh(mesh.devices.reshape(groups, -1, 4, 2), ("grp",) + SUB)
    specs = (
        P("grp", SUB, None, None),
        P("grp", SUB, None),
        P("grp", SUB, None, None, None, None),
        P("grp", SUB, None, None),
        P("grp", SUB, None, None),
        P("grp", SUB, None, None),
        P("grp", SUB, None),
    )
    return jax.shard_map(
        per_device, mesh=split, in_specs=specs, out_specs=P("grp", SUB, None, None), check_vma=False
    )
```

time: 1000 us -> 278 us (0.28)
  blocking collectives: 828 us -> 115 us
  local copies, waits for them, and re-layouts: 74.2 us -> 52.7 us
  starting transfers between devices: 25.8 us -> 42 us
  waiting for transfers between devices: 0.03 us -> 13.2 us
    psum x4 -> x0, blocking collectives: 503 us -> none  [global_sums(): return lax.psum(values, ('grp', 'sub'))]
    all_gather x4 -> x6, blocking collectives: 325 us -> 25.3 us  [the longest x3 19.4 us: gather_coarse(): pair = lax.all_gather(piece, 'core', axis=1, tiled=True)]
    all_to_all x0 -> x7, blocking collectives: none -> 89.6 us  [gathered(): lax.all_to_all(jnp.broadcast_to(value[None], (size,) + value.shape), axis...]
    all_to_all x0 -> x2, waiting for transfers between devices: none -> 10.5 us  [gathered(): lax.all_to_all(jnp.broadcast_to(value[None], (size,) + value.shape), axis...]
    all_to_all x0 -> x2, starting transfers between devices: none -> 10 us  [gathered(): lax.all_to_all(jnp.broadcast_to(value[None], (size,) + value.shape), axis...]
    ppermute x12 -> x9, starting transfers between devices: 25.8 us -> 32 us  [the longest x3 16.9 us: exchange(): other = lax.ppermute(jnp.where(first, rims[:, 2], rims[:, 3]), SUB, across)]
    reshape x15 -> x12, local copies, waits for them, and re-layouts: 23.3 us -> 19.4 us  [the longest x6 8.97 us: local_part(): picked = field.reshape(count, nblocks, rows // nblocks)[:, pattern]]
    dot_general x15 -> x12, matrix products: 31.8 us -> 28.2 us  [the longest x3 13.3 us: local_part(): jnp.einsum('bkoi,nbki->nbo', blocks, picked, precision=HIGH)]
  transfers between devices with their start and end apart: 12 -> 11, of which waited for: 0 -> 4; matrix products, arithmetic and copies ran while one was open for 3% -> 12% of each run, Pallas kernels for 0% -> 0%
where the time goes in v1:
time: 278 us; the launch traced here: 274 us
  blocking collectives  115 us (41%)
  local copies, waits for them, and re-layouts  52.7 us (19%)
  starting transfers between devices  42 us (15%)
  matrix products  28.2 us (10%)
  other arithmetic  22.7 us (8%)
  waiting for transfers between devices  13.2 us (5%)
    all_to_all x7, blocking collectives, gathered(): lax.all_to_all(jnp.broadcast_to(value[None], (size,) + value.shape), axis...  89.6 us
    all_gather x3, blocking collectives, gather_coarse(): pair = lax.all_gather(piece, 'core', axis=1, tiled=True)  19.4 us
    ppermute x3, starting transfers between devices, exchange(): other = lax.ppermute(jnp.where(first, rims[:, 2], rims[:, 3]), SUB, across)  16.9 us
    dot_general x3, matrix products, local_part(): jnp.einsum('bkoi,nbki->nbo', blocks, picked, precision=HIGH)  13.3 us
    ppermute x3, starting transfers between devices, exchange(): from_low = lax.ppermute(rims[:, 1], 'grp', up)  11.3 us
    all_to_all x2, waiting for transfers between devices, gathered(): lax.all_to_all(jnp.broadcast_to(value[None], (size,) + value.shape), axis...  10.5 us
    all_to_all x2, starting transfers between devices, gathered(): lax.all_to_all(jnp.broadcast_to(value[None], (size,) + value.shape), axis...  10 us
    reshape x6, local copies, waits for them, and re-layouts, local_part(): picked = field.reshape(count, nblocks, rows // nblocks)[:, pattern]  8.97 us
  transfers between devices with their start and end apart: 11, of which 4 were waited for; matrix products, arithmetic and copies ran while one was open for 12% of the time, Pallas kernels for 0%

profile of v1, /device:TPU:1, one launch (start us, length us, event | category | flops | bytes accessed | tf_op | source)
XLA Modules:
  0.0 274.0 jit_solution(18038995366985373508)
XLA Ops:
  1.6 15.7 %all-gather.3 = f32[2,48,8]{1,2,0:T(8,128)S(1)} all-gather(f32[1,48,8]{1,2,0:T(8,128)S(1)} %convolution_bitcast_fusion.2), channel_id=1, replica_groups=mesh['grp'=8,'z'=16,'x'=4,'core'=2] {'core'}, dimensions={0}, use_global_device_ids=true | all-gather | bytes 4608 | tf_op jit(solution)/shard_map/all_gather | solution.py:18
  19.2 6.0 %all-to-all-start = ((f32[16,8,96]{2,1,0:T(8,128)}), f32[16,8,96]{2,1,0:T(8,128)}, u32[]{:S(2)}, u32[]{:S(2)}) async-start(f32[16,8,96]{2,1,0:T(8,128)} %broadcast_in_dim.20), calls=%async_computation | async-start | bytes 131072 | tf_op jit(solution)/shard_map/all_to_all | solution.py:13
  28.5 8.4 %all-to-all-done = f32[16,8,96]{2,1,0:T(8,128)} async-done(((f32[16,8,96]{2,1,0:T(8,128)}), f32[16,8,96]{2,1,0:T(8,128)}, u32[]{:S(2)}, u32[]{:S(2)}) %all-to-all-start) | async-done | bytes 49184 | tf_op jit(solution)/shard_map/all_to_all | solution.py:13
  38.5 4.0 %all-to-all-start.1 = ((f32[4,16,8,96]{3,1,2,0:T(8,128)}), f32[4,16,8,96]{3,1,2,0:T(8,128)}, u32[]{:S(2)}, u32[]{:S(2)}) async-start(f32[4,16,8,96]{3,1,2,0:T(8,128)} %broadcast_in_dim.21), calls=%async_computation.1 | async-start | bytes 524288 | tf_op jit(solution)/shard_map/all_to_all | solution.py:13
  46.0 2.1 all-to-all-done.1
  51.8 2.4 fusion.10
  57.6 2.0 gather_fusion.1
  61.0 5.5 %collective-permute-start.2 = (f32[8,512]{1,0:T(8,128)}, f32[8,512]{1,0:T(8,128)}, u32[]{:S(2)}, u32[]{:S(2)}) collective-permute-start(f32[8,512]{1,0:T(8,128)} %get-tuple-element.52), channel_id=1, source_target_pairs={{1,2},{2,1},{3,4},{4,3},{5,6},{6,5},{7,8},{8,7},{9,10},{10,9},{11,... | collective-permute-start | bytes 49160 | tf_op jit(solution)/shard_map/ppermute | solution.py:111
  66.6 3.8 %collective-permute-start = (f32[8,512]{1,0:T(8,128)}, f32[8,512]{1,0:T(8,128)}, u32[]{:S(2)}, u32[]{:S(2)}) collective-permute-start(f32[8,512]{1,0:T(8,128)} %get-tuple-element.51), channel_id=1, source_target_pairs={{0,128},{128,256},{256,384},{384,512},{512,640},{640,768},{768,896... | collective-permute-start | bytes 49160 | tf_op jit(solution)/shard_map/ppermute | solution.py:108
  73.3 2.3 gather_fusion
  75.5 4.4 %fusion.12 = f32[8,32,64]{2,0,1:T(8,128)S(1)} fusion(f32[8,32,3,64]{3,0,2,1:T(8,128)} %bitcast.220, f32[1,1,32,3,64,64]{5,4,3,2,1,0:T(8,128)S(1)} %copy-done), kind=kOutput, calls=%fused_computation.24 | convolution fusion | flops 37748736 | bytes 1835008 | tf_op jit(solution)/shard_map/bkoi,nbki->nbo/dot_general | solution.py:96
  82.3 2.0 all-gather
  87.1 2.5 scatter_fusion
  96.0 14.8 %all_to_all.45 = f32[16,8,96]{2,1,0:T(8,128)S(1)} all-to-all(f32[16,8,96]{2,1,0:T(8,128)S(1)} %broadcast_in_dim.22), channel_id=1, replica_groups=mesh['grp'=8,'z'=16,'x'=4,'core'=2] {'z'}, dimensions={0} | all-to-all | bytes 98304 | tf_op jit(solution)/shard_map/all_to_all | solution.py:13
  110.8 10.1 %all_to_all.46 = f32[4,16,8,96]{3,1,2,0:T(8,128)S(1)} all-to-all(f32[4,16,8,96]{3,1,2,0:T(8,128)S(1)} %broadcast_in_dim.23), channel_id=1, replica_groups=mesh['grp'=8,'z'=16,'x'=4,'core'=2] {'x'}, dimensions={0} | all-to-all | bytes 393216 | tf_op jit(solution)/shard_map/all_to_all | solution.py:13
  123.7 2.4 fusion.8
  131.0 2.3 gather_fusion.2
  136.7 5.7 %collective-permute-start.5 = (f32[8,512]{1,0:T(8,128)}, f32[8,512]{1,0:T(8,128)}, u32[]{:S(2)}, u32[]{:S(2)}) collective-permute-start(f32[8,512]{1,0:T(8,128)} %get-tuple-element.48), channel_id=1, source_target_pairs={{1,2},{2,1},{3,4},{4,3},{5,6},{6,5},{7,8},{8,7},{9,10},{10,9},{11,... | collective-permute-start | bytes 49160 | tf_op jit(solution)/shard_map/ppermute | solution.py:111
  142.4 4.4 %fusion.15 = f32[8,32,64]{2,0,1:T(8,128)S(1)} fusion(f32[8,32,3,64]{3,0,2,1:T(8,128)} %bitcast.219, f32[1,1,32,3,64,64]{5,4,3,2,1,0:T(8,128)S(1)} %copy-done), kind=kOutput, calls=%fused_computation.25 | convolution fusion | flops 37748736 | bytes 1835008 | tf_op jit(solution)/shard_map/bkoi,nbki->nbo/dot_general | solution.py:96
  149.1 4.0 %collective-permute-start.3 = (f32[8,512]{1,0:T(8,128)}, f32[8,512]{1,0:T(8,128)S(1)}, u32[]{:S(2)}, u32[]{:S(2)}) collective-permute-start(f32[8,512]{1,0:T(8,128)} %get-tuple-element.47), channel_id=1, source_target_pairs={{0,128},{128,256},{256,384},{384,512},{512,640},{640,768},{768,896... | collective-permute-start | bytes 49160 | tf_op jit(solution)/shard_map/ppermute | solution.py:108
  154.4 2.0 all-gather.1
  159.1 2.5 scatter_fusion.1
  168.1 16.0 %all_to_all.47 = f32[16,8,96]{2,1,0:T(8,128)S(1)} all-to-all(f32[16,8,96]{2,1,0:T(8,128)S(1)} %broadcast_in_dim.24), channel_id=1, replica_groups=mesh['grp'=8,'z'=16,'x'=4,'core'=2] {'z'}, dimensions={0} | all-to-all | bytes 98304 | tf_op jit(solution)/shard_map/all_to_all | solution.py:13
  184.1 8.9 %all_to_all.48 = f32[4,16,8,96]{3,1,2,0:T(8,128)S(1)} all-to-all(f32[4,16,8,96]{3,1,2,0:T(8,128)S(1)} %broadcast_in_dim.25), channel_id=1, replica_groups=mesh['grp'=8,'z'=16,'x'=4,'core'=2] {'x'}, dimensions={0} | all-to-all | bytes 393216 | tf_op jit(solution)/shard_map/all_to_all | solution.py:13
  195.8 2.4 fusion.6
  206.0 5.6 %collective-permute-start.8 = (f32[8,512]{1,0:T(8,128)}, f32[8,512]{1,0:T(8,128)}, u32[]{:S(2)}, u32[]{:S(2)}) collective-permute-start(f32[8,512]{1,0:T(8,128)} %get-tuple-element.44), channel_id=1, source_target_pairs={{1,2},{2,1},{3,4},{4,3},{5,6},{6,5},{7,8},{8,7},{9,10},{10,9},{11,... | collective-permute-start | bytes 49160 | tf_op jit(solution)/shard_map/ppermute | solution.py:111
  211.7 4.4 %fusion.18 = f32[8,32,64]{2,0,1:T(8,128)S(1)} fusion(f32[8,32,3,64]{3,0,2,1:T(8,128)} %bitcast.218, f32[1,1,32,3,64,64]{5,4,3,2,1,0:T(8,128)S(1)} %copy-done), kind=kOutput, calls=%fused_computation.26 | convolution fusion | flops 37748736 | bytes 1835008 | tf_op jit(solution)/shard_map/bkoi,nbki->nbo/dot_general | solution.py:96
  218.4 3.5 %collective-permute-start.6 = (f32[8,512]{1,0:T(8,128)}, f32[8,512]{1,0:T(8,128)S(1)}, u32[]{:S(2)}, u32[]{:S(2)}) collective-permute-start(f32[8,512]{1,0:T(8,128)} %get-tuple-element.43), channel_id=1, source_target_pairs={{0,128},{128,256},{256,384},{384,512},{512,640},{640,768},{768,896... | collective-permute-start | bytes 49160 | tf_op jit(solution)/shard_map/ppermute | solution.py:108
  225.8 2.0 collective-permute-done.7
  232.9 9.1 %all_to_all.49 = f32[8,10,8]{1,2,0:T(8,128)S(1)} all-to-all(f32[8,10,8]{1,2,0:T(8,128)S(1)} %broadcast_in_dim.26), channel_id=1, replica_groups=mesh['grp'=8,'z'=16,'x'=4,'core'=2] {'x','core'}, dimensions={0} | all-to-all | bytes 5120 | tf_op jit(solution)/shard_map/all_to_all | solution.py:13
  242.0 15.5 %all_to_all.50 = f32[16,10,8]{1,2,0:T(8,128)S(1)} all-to-all(f32[16,10,8]{1,2,0:T(8,128)S(1)} %broadcast_in_dim.27), channel_id=1, replica_groups=mesh['grp'=8,'z'=16,'x'=4,'core'=2] {'z'}, dimensions={0} | all-to-all | bytes 10240 | tf_op jit(solution)/shard_map/all_to_all | solution.py:13
  257.5 15.3 %all_to_all.51 = f32[8,10,8]{1,2,0:T(8,128)S(1)} all-to-all(f32[8,10,8]{1,2,0:T(8,128)S(1)} %broadcast_in_dim.28), channel_id=1, replica_groups=mesh['grp'=8,'z'=16,'x'=4,'core'=2] {'grp'}, dimensions={0} | all-to-all | bytes 5120 | tf_op jit(solution)/shard_map/all_to_all | solution.py:13
  (117 shorter events, 81.6 us)
Async XLA Ops:
  0.0 75.5 %copy-start = (f32[1,1,32,3,64,64]{5,4,3,2,1,0:T(8,128)S(1)}, f32[1,1,32,3,64,64]{5,4,3,2,1,0:T(8,128)}, u32[]{:S(2)}) copy-start(f32[1,1,32,3,64,64]{5,4,3,2,1,0:T(8,128)} %param.9) | copy-start | bytes 4718596
  0.0 54.2 %copy-start.1 = (f32[1,1,48,2048]{3,2,1,0:T(8,128)S(1)}, f32[1,1,48,2048]{3,2,1,0:T(8,128)}, u32[]{:S(2)}) copy-start(f32[1,1,48,2048]{3,2,1,0:T(8,128)} %param.12) | copy-start | bytes 1179652
  0.0 54.2 %copy-start.9 = (f32[1,1,2048]{2,1,0:T(1,128)S(1)}, f32[1,1,2048]{2,1,0:T(1,128)}, u32[]{:S(2)}) copy-start(f32[1,1,2048]{2,1,0:T(1,128)} %param.8) | copy-start | bytes 24580
  19.2 17.7 %all-to-all-start = ((f32[16,8,96]{2,1,0:T(8,128)}), f32[16,8,96]{2,1,0:T(8,128)}, u32[]{:S(2)}, u32[]{:S(2)}) async-start(f32[16,8,96]{2,1,0:T(8,128)} %broadcast_in_dim.20), calls=%async_computation | async-start | bytes 131072 | tf_op jit(solution)/shard_map/all_to_all | solution.py:13
  38.5 9.6 %all-to-all-start.1 = ((f32[4,16,8,96]{3,1,2,0:T(8,128)}), f32[4,16,8,96]{3,1,2,0:T(8,128)}, u32[]{:S(2)}, u32[]{:S(2)}) async-start(f32[4,16,8,96]{3,1,2,0:T(8,128)} %broadcast_in_dim.21), calls=%async_computation.1 | async-start | bytes 524288 | tf_op jit(solution)/shard_map/all_to_all | solution.py:13
  61.0 23.3 %collective-permute-start.2 = (f32[8,512]{1,0:T(8,128)}, f32[8,512]{1,0:T(8,128)}, u32[]{:S(2)}, u32[]{:S(2)}) collective-permute-start(f32[8,512]{1,0:T(8,128)} %get-tuple-element.52), channel_id=1, source_target_pairs={{1,2},{2,1},{3,4},{4,3},{5,6},{6,5},{7,8},{8,7},{9,10},{10,9},{11,... | collective-permute-start | bytes 49160 | tf_op jit(solution)/shard_map/ppermute | solution.py:111
  66.6 18.5 %collective-permute-start = (f32[8,512]{1,0:T(8,128)}, f32[8,512]{1,0:T(8,128)}, u32[]{:S(2)}, u32[]{:S(2)}) collective-permute-start(f32[8,512]{1,0:T(8,128)} %get-tuple-element.51), channel_id=1, source_target_pairs={{0,128},{128,256},{256,384},{384,512},{512,640},{640,768},{768,896... | collective-permute-start | bytes 49160 | tf_op jit(solution)/shard_map/ppermute | solution.py:108
  70.4 14.7 %collective-permute-start.1 = (f32[8,512]{1,0:T(8,128)}, f32[8,512]{1,0:T(8,128)}, u32[]{:S(2)}, u32[]{:S(2)}) collective-permute-start(f32[8,512]{1,0:T(8,128)} %get-tuple-element.54), channel_id=1, source_target_pairs={{128,0},{256,128},{384,256},{512,384},{640,512},{768,640},{896,768... | collective-permute-start | bytes 49160 | tf_op jit(solution)/shard_map/ppermute | solution.py:109
  90.5 0.6 copy-start.5
  136.7 19.8 %collective-permute-start.5 = (f32[8,512]{1,0:T(8,128)}, f32[8,512]{1,0:T(8,128)}, u32[]{:S(2)}, u32[]{:S(2)}) collective-permute-start(f32[8,512]{1,0:T(8,128)} %get-tuple-element.48), channel_id=1, source_target_pairs={{1,2},{2,1},{3,4},{4,3},{5,6},{6,5},{7,8},{8,7},{9,10},{10,9},{11,... | collective-permute-start | bytes 49160 | tf_op jit(solution)/shard_map/ppermute | solution.py:111
  149.1 8.1 %collective-permute-start.3 = (f32[8,512]{1,0:T(8,128)}, f32[8,512]{1,0:T(8,128)S(1)}, u32[]{:S(2)}, u32[]{:S(2)}) collective-permute-start(f32[8,512]{1,0:T(8,128)} %get-tuple-element.47), channel_id=1, source_target_pairs={{0,128},{128,256},{256,384},{384,512},{512,640},{640,768},{768,896... | collective-permute-start | bytes 49160 | tf_op jit(solution)/shard_map/ppermute | solution.py:108
  153.1 4.7 %collective-permute-start.4 = (f32[8,512]{1,0:T(8,128)}, f32[8,512]{1,0:T(8,128)S(1)}, u32[]{:S(2)}, u32[]{:S(2)}) collective-permute-start(f32[8,512]{1,0:T(8,128)} %get-tuple-element.50), channel_id=1, source_target_pairs={{128,0},{256,128},{384,256},{512,384},{640,512},{768,640},{896,768... | collective-permute-start | bytes 49160 | tf_op jit(solution)/shard_map/ppermute | solution.py:109
  162.5 0.6 copy-start.7
  201.5 28.8 %copy-start.4 = (f32[8,2048]{1,0:T(8,128)S(1)}, f32[8,2048]{1,0:T(8,128)}, u32[]{:S(2)}) copy-start(f32[8,2048]{1,0:T(8,128)} %convolution_add_fusion) | copy-start | bytes 196612
  201.5 28.8 %copy-start.6 = (f32[8,2048]{1,0:T(8,128)S(1)}, f32[8,2048]{1,0:T(8,128)}, u32[]{:S(2)}) copy-start(f32[8,2048]{1,0:T(8,128)} %copy-done.5) | copy-start | bytes 196612
  201.5 28.8 %copy-start.8 = (f32[8,2048]{1,0:T(8,128)S(1)}, f32[8,2048]{1,0:T(8,128)}, u32[]{:S(2)}) copy-start(f32[8,2048]{1,0:T(8,128)} %copy-done.7) | copy-start | bytes 196612
  204.0 69.3 %copy-start.2 = (f32[8,2048]{1,0:T(8,128)S(1)}, f32[8,2048]{1,0:T(8,128)}, u32[]{:S(2)}) copy-start(f32[8,2048]{1,0:T(8,128)} %convolution_add_fusion.2) | copy-start | bytes 196612
  204.0 69.3 %copy-start.3 = (f32[8,2048]{1,0:T(8,128)S(1)}, f32[8,2048]{1,0:T(8,128)}, u32[]{:S(2)}) copy-start(f32[8,2048]{1,0:T(8,128)} %convolution_add_fusion.1) | copy-start | bytes 196612
  206.0 17.2 %copy-start.10 = (f32[8,1,512]{2,0,1:T(8,128)S(1)}, f32[8,1,512]{2,0,1:T(8,128)}, u32[]{:S(2)}) copy-start(f32[8,1,512]{2,0,1:T(8,128)} %get-tuple-element.45) | copy-start | bytes 49156
  206.0 19.1 %collective-permute-start.8 = (f32[8,512]{1,0:T(8,128)}, f32[8,512]{1,0:T(8,128)}, u32[]{:S(2)}, u32[]{:S(2)}) collective-permute-start(f32[8,512]{1,0:T(8,128)} %get-tuple-element.44), channel_id=1, source_target_pairs={{1,2},{2,1},{3,4},{4,3},{5,6},{6,5},{7,8},{8,7},{9,10},{10,9},{11,... | collective-permute-start | bytes 49160 | tf_op jit(solution)/shard_map/ppermute | solution.py:111
  218.4 7.4 %collective-permute-start.6 = (f32[8,512]{1,0:T(8,128)}, f32[8,512]{1,0:T(8,128)S(1)}, u32[]{:S(2)}, u32[]{:S(2)}) collective-permute-start(f32[8,512]{1,0:T(8,128)} %get-tuple-element.43), channel_id=1, source_target_pairs={{0,128},{128,256},{256,384},{384,512},{512,640},{640,768},{768,896... | collective-permute-start | bytes 49160 | tf_op jit(solution)/shard_map/ppermute | solution.py:108
  221.9 5.9 %collective-permute-start.7 = (f32[8,512]{1,0:T(8,128)}, f32[8,512]{1,0:T(8,128)S(1)}, u32[]{:S(2)}, u32[]{:S(2)}) collective-permute-start(f32[8,512]{1,0:T(8,128)} %get-tuple-element.46), channel_id=1, source_target_pairs={{128,0},{256,128},{384,256},{512,384},{640,512},{768,640},{896,768... | collective-permute-start | bytes 49160 | tf_op jit(solution)/shard_map/ppermute | solution.py:109

commit v2 on v1

v2 whole, which is shorter than its diff:
```python
import functools

import jax
import jax.numpy as jnp
from jax import lax
from jax.experimental import pallas as pl
from jax.experimental.pallas import tpu as pltpu
from jax.sharding import Mesh, PartitionSpec as P

ITERS = 3
SUB = ("z", "x", "core")
SHRINK = 1.0 / 256.0
F32 = jnp.float32
BF16 = jnp.bfloat16
HALF = 64
LANES = 128


def vmem():
    return pl.BlockSpec(memory_space=pltpu.VMEM)


def smem():
    return pl.BlockSpec(memory_space=pltpu.SMEM)


def call(body, outs, specs, flops, nbytes, scratch=()):
    return pl.pallas_call(
        body,
        out_shape=outs,
        in_specs=specs,
        out_specs=jax.tree.map(lambda _: vmem(), outs),
        scratch_shapes=scratch,
        compiler_params=pltpu.CompilerParams(vmem_limit_bytes=40 * 1024 * 1024),
        cost_estimate=pl.CostEstimate(flops=flops, bytes_accessed=nbytes, transcendentals=0),
    )


def halves(value):
    high = value.astype(BF16).astype(F32)
    return high, value - high


def stacked(value):
    high, low = halves(value)
    return jnp.concatenate([high, low], axis=0).astype(BF16)


def lane_of(shape):
    return lax.broadcasted_iota(jnp.int32, shape, len(shape) - 1)


def coarse_piece(field, basis_t, core):
    count = field.shape[0]
    out = jnp.dot(stacked(field), basis_t, preferred_element_type=F32)
    lane = lane_of((count, LANES))
    part = out[:count] + jnp.where(lane < HALF, out[count:], 0.0)
    both = part + pltpu.roll(part, HALF, 1)
    start = core * HALF
    return jnp.where((lane >= start) & (lane < start + 48), both, 0.0)


def transposed_halves(value):
    high, low = halves(value)
    rows, width = value.shape
    parts = [high, low]
    if rows < HALF:
        pad = jnp.zeros((HALF - rows, width), F32)
        parts = [high, pad, low, pad]
    return jnp.concatenate(parts, axis=0).T.astype(BF16)


def start_kernel(core_ref, rhs_ref, basis_ref, diag_ref, basis_t_ref, basis_h_ref, inv_ref, piece_ref):
    rows = basis_ref.shape[1]
    for t in range(rows // LANES):
        cols = slice(t * LANES, (t + 1) * LANES)
        basis_t_ref[cols, :] = transposed_halves(basis_ref[:, cols])
    high, low = halves(basis_ref[...])
    basis_h_ref[:, :rows] = high.astype(BF16)
    basis_h_ref[:, rows:] = low.astype(BF16)
    inv_ref[...] = 1.0 / diag_ref[...]
    piece = coarse_piece(rhs_ref[...], basis_t_ref[...], core_ref[0])
    for z in range(piece_ref.shape[0]):
        piece_ref[z] = piece


def coarse_kernel(inverse_ref, out_ref):
    gen, total = inverse_ref.shape
    zero = jnp.zeros((HALF - gen, LANES), BF16)
    for t in range(total // (2 * gen)):
        part = transposed_halves(inverse_ref[:, t * 2 * gen : (t + 1) * 2 * gen])
        row = t * LANES
        out_ref[row : row + gen, :] = part[:gen]
        out_ref[row + gen : row + HALF, :] = zero
        out_ref[row + HALF : row + HALF + gen, :] = part[gen:]
        out_ref[row + HALF + gen : row + LANES, :] = zero


def block_kernel(blocks_ref, out_ref):
    nblocks, knz, blk, _ = blocks_ref.shape
    zero = jnp.zeros((blk, LANES), BF16)

    def step(b, carry):
        for odd in range(2):
            at = 2 * b + odd
            for k in range(knz):
                high, low = halves(blocks_ref[at, k])
                pair = [low, high] if odd else [high, low]
                out_ref[at, k * blk : (k + 1) * blk, :] = (
                    jnp.concatenate(pair, axis=0).T.astype(BF16)
                )
            out_ref[at, knz * blk :, :] = zero
        return carry

    lax.fori_loop(0, nblocks // 2, step, 0)


def field_kernel(
    core_ref, margin_ref, pieces_ref, k_ref, inv_ref, coarse_ref, basis_h_ref,
    p_ref, up_ref, down_ref, across_ref, partner_ref, packed_ref,
):
    count, rows = k_ref.shape
    _, xs, zs, _, _ = pieces_ref.shape
    for z in range(zs):
        for x in range(xs):
            t = z * xs + x
            packed_ref[:, t * LANES : (t + 1) * LANES] = stacked(
                pieces_ref[0, x, z] + pieces_ref[1, x, z]
            )
    out = jnp.dot(packed_ref[...], coarse_ref[...], preferred_element_type=F32)
    part = out[:count] + jnp.where(lane_of((count, LANES)) < HALF, out[count:], 0.0)
    answer = part + pltpu.roll(part, HALF, 1)
    back = jnp.dot(stacked(answer[:, :48]), basis_h_ref[...], preferred_element_type=F32)
    p_ref[...] = (
        k_ref[...] * inv_ref[...] + (back[:count, :rows] + back[count:, :rows]) + back[:count, rows:]
    )
    core = core_ref[0]
    for rim_ref, d in ((up_ref, 1), (down_ref, 0), (across_ref, 2 + core), (partner_ref, 3 - core)):
        for j in range(margin_ref.shape[1]):
            tile = margin_ref[d, j]
            rim_ref[:, j * LANES : (j + 1) * LANES] = p_ref[
                :, pl.ds(pl.multiple_of(tile * LANES, LANES), LANES)
            ]


def local_kernel(pattern_ref, p_ref, diag_ref, weights_ref, out_ref, left_ref, right_ref):
    count, rows = p_ref.shape
    lane = lane_of((2 * count, LANES))
    low_half = lane < HALF
    for t in range(rows // LANES):
        tile = p_ref[:, t * LANES : (t + 1) * LANES]
        high, low = halves(tile)
        both = jnp.concatenate([high, low], axis=0)
        turned = pltpu.roll(both, HALF, 1)
        left_ref[2 * t] = jnp.where(low_half, both, 0.0).astype(BF16)
        left_ref[2 * t + 1] = jnp.where(low_half, turned, 0.0).astype(BF16)
        right_ref[2 * t] = jnp.where(low_half, 0.0, turned).astype(BF16)
        right_ref[2 * t + 1] = jnp.where(low_half, 0.0, both).astype(BF16)
    lower = lane_of((count, LANES)) < HALF

    def product(b):
        first = left_ref[pattern_ref[b, 0]] + right_ref[pattern_ref[b, 1]]
        x = jnp.concatenate([first, left_ref[pattern_ref[b, 2]]], axis=1)
        return jnp.dot(x, weights_ref[b], preferred_element_type=F32)

    for t in range(rows // LANES):
        cols = slice(t * LANES, (t + 1) * LANES)
        even, odd = product(2 * t), product(2 * t + 1)
        even = even[:count] + jnp.where(lower, even[count:], 0.0)
        odd = odd[:count] + jnp.where(lower, 0.0, odd[count:])
        local = jnp.where(lower, even, odd) + pltpu.roll(jnp.where(lower, odd, even), HALF, 1)
        out_ref[:, cols] = diag_ref[:, cols] * p_ref[:, cols] + local


def couple(core_ref, margin_ref, base_ref, low_ref, high_ref, across_ref, both_ref, k_ref):
    core = core_ref[0]
    k_ref[...] = base_ref[...]
    for d, source in ((0, low_ref), (1, high_ref), (2 + core, across_ref), (3 - core, both_ref.at[1 - core])):
        for j in range(margin_ref.shape[1]):
            at = pl.ds(pl.multiple_of(margin_ref[d, j] * LANES, LANES), LANES)
            k_ref[:, at] = k_ref[:, at] - source[:, j * LANES : (j + 1) * LANES]
    k_ref[...] = k_ref[...] * SHRINK


def next_kernel(
    core_ref, margin_ref, base_ref, low_ref, high_ref, across_ref, both_ref, basis_t_ref,
    k_ref, piece_ref,
):
    couple(core_ref, margin_ref, base_ref, low_ref, high_ref, across_ref, both_ref, k_ref)
    piece = coarse_piece(k_ref[...], basis_t_ref[...], core_ref[0])
    for z in range(piece_ref.shape[0]):
        piece_ref[z] = piece


def gram_kernel(
    core_ref, margin_ref, base_ref, low_ref, high_ref, across_ref, both_ref, k0_ref, k1_ref, k2_ref,
    sums_ref, k3_ref,
):
    couple(core_ref, margin_ref, base_ref, low_ref, high_ref, across_ref, both_ref, k3_ref)
    fields = [k0_ref[...], k1_ref[...], k2_ref[...], k3_ref[...]]
    count = fields[0].shape[0]
    lane = lane_of((count, LANES))
    sums = jnp.zeros((count, LANES), F32)
    for at, (i, j) in enumerate(PAIRS):
        sums = jnp.where(lane == at, jnp.sum(fields[i] * fields[j], axis=1, keepdims=True), sums)
    for n in range(sums_ref.shape[0]):
        sums_ref[n] = sums


PAIRS = [(i, j) for j in range(ITERS + 1) for i in range(j + 1)]


def spread(value, axis):
    return lax.all_to_all(value, axis, 0, 0)


def repeated(value, axis):
    return jnp.broadcast_to(value[None], (lax.axis_size(axis),) + value.shape)


def gather_coarse(piece):
    column = spread(piece, "z")
    return lax.all_gather(spread(repeated(column, "x"), "x"), "core")


def total(values):
    part = jnp.sum(spread(values, ("x", "core")), axis=0)
    part = jnp.sum(spread(repeated(part, "z"), "z"), axis=0)
    return jnp.sum(spread(repeated(part, "grp"), "grp"), axis=0)


def least_squares(columns, beta):
    ortho = []
    upper = []
    for k in range(len(columns)):
        vector = columns[k]
        coeffs = []
        for i in range(k):
            weight = sum(a * b for a, b in zip(ortho[i], columns[k]))
            coeffs.append(weight)
            vector = [a - weight * b for a, b in zip(vector, ortho[i])]
        length = jnp.sqrt(sum(a * a for a in vector))
        coeffs.append(length)
        upper.append(coeffs)
        ortho.append([a / length for a in vector])
    result = [None] * len(columns)
    for k in reversed(range(len(columns))):
        value = ortho[k][0] * beta
        for i in range(k + 1, len(columns)):
            value = value - upper[i][k] * result[i]
        result[k] = value / upper[k][k]
    return result


def combine(gram):
    size = ITERS + 1
    full = [[gram[min(i, j)][max(i, j)] for j in range(size)] for i in range(size)]
    zero = jnp.zeros_like(full[0][0])

    def inner(a, b):
        return sum(
            a[i] * sum(full[i][j] * b[j] for j in range(size) if b[j] is not None)
            for i in range(size)
            if a[i] is not None
        )

    beta = jnp.sqrt(full[0][0])
    vectors = [[1.0 / beta] + [None] * ITERS]
    columns = []
    for step in range(ITERS):
        image = [None] + [None if c is None else c * (1.0 / SHRINK) for c in vectors[step][:ITERS]]
        square = inner(image, image)
        dots = [inner(vec, image) for vec in vectors]
        heights = sum(d * d for d in dots)
        height = jnp.sqrt(jnp.maximum(square - heights, 0.001 * square))
        columns.append(dots + [height] + [zero] * (ITERS - step - 1))
        rest = []
        for m in range(size):
            terms = [(dots[i], vectors[i][m]) for i in range(step + 1) if vectors[i][m] is not None]
            if image[m] is None and not terms:
                rest.append(None)
                continue
            value = zero if image[m] is None else image[m]
            for dot, factor in terms:
                value = value - dot * factor
            rest.append(value / height)
        vectors.append(rest)
    weights = least_squares(columns, beta)
    return [
        sum(weights[i] * vectors[i][m] for i in range(ITERS) if vectors[i][m] is not None)
        for m in range(ITERS)
    ]


def shape(*dims, dtype=F32):
    return jax.ShapeDtypeStruct(dims, dtype)


def per_device(rhs, diagonal, blocks, pattern, margin, basis, coarse_inverse):
    source = rhs[0, 0]
    diag_row = diagonal[0]
    pattern = pattern[0, 0]
    margin = margin[0, 0]
    basis = basis[0, 0]
    inverse = coarse_inverse[0]
    count, rows = source.shape
    gen = basis.shape[0]
    nblocks, knz = pattern.shape
    groups, zs, xs = lax.axis_size("grp"), lax.axis_size("z"), lax.axis_size("x")
    subs = lax.axis_size(SUB)
    rim = margin.shape[1] * LANES
    core = lax.axis_index("core").astype(jnp.int32).reshape(1)
    up = [(i, i + 1) for i in range(groups - 1)]
    down = [(j, i) for i, j in up]
    across = [(i, ((i + 1) ^ 1) - 1) for i in range(1, subs - 1)]
    wide = subs * HALF

    basis_t, basis_h, inv_row, piece = call(
        start_kernel,
        [shape(rows, LANES, dtype=BF16), shape(gen, 2 * rows, dtype=BF16), shape(1, rows), shape(zs, count, LANES)],
        [smem(), vmem(), vmem(), vmem()],
        3_000_000,
        1_500_000,
    )(core, source, basis, diag_row)
    coarse = call(coarse_kernel, shape(wide, LANES, dtype=BF16), [vmem()], 1_000_000, 3_200_000)(inverse)
    weights = call(
        block_kernel, shape(nblocks, 4 * HALF, LANES, dtype=BF16), [vmem()], 1_000_000, 5_000_000
    )(blocks[0, 0])

    krylov = [source]
    conditioned = []
    sums = None
    for step in range(ITERS):
        pieces = gather_coarse(piece)
        p, send_up, send_down, send_across, send_partner = call(
            field_kernel,
            [shape(count, rows)] + [shape(count, rim)] * 4,
            [smem(), smem()] + [vmem()] * 5,
            8_000_000,
            3_500_000,
            [pltpu.VMEM((2 * count, wide), BF16)],
        )(core, margin, pieces, krylov[-1], inv_row, coarse, basis_h)
        conditioned.append(p)
        from_low = lax.ppermute(send_up, "grp", up)
        from_high = lax.ppermute(send_down, "grp", down)
        other = lax.ppermute(send_across, SUB, across)
        partner = lax.all_gather(send_partner, "core")
        base = call(
            local_kernel,
            shape(count, rows),
            [smem()] + [vmem()] * 3,
            20_000_000,
            2_500_000,
            [pltpu.VMEM((nblocks, 2 * count, LANES), BF16)] * 2,
        )(pattern, p, diag_row, weights)
        shared = (core, margin, base, from_low, from_high, other, partner)
        if step < ITERS - 1:
            field, piece = call(
                next_kernel,
                [shape(count, rows), shape(zs, count, LANES)],
                [smem(), smem()] + [vmem()] * 6,
                4_000_000,
                1_000_000,
            )(*shared, basis_t)
            krylov.append(field)
        else:
            sums = call(
                gram_kernel,
                shape(2 * xs, count, LANES),
                [smem(), smem()] + [vmem()] * 8,
                400_000,
                500_000,
                [pltpu.VMEM((count, rows), F32)],
            )(*shared, *krylov)
    sums = total(sums)
    gram = [[None] * (ITERS + 1) for _ in range(ITERS + 1)]
    for at, (i, j) in enumerate(PAIRS):
        gram[i][j] = sums[:, at : at + 1]
    factors = combine(gram)
    result = sum(f * p for f, p in zip(factors, conditioned))
    return result[None, None]


def solution(mesh):
    groups = mesh.shape["grp"]
    split = Mesh(mesh.devices.reshape(groups, -1, 4, 2), ("grp",) + SUB)
    specs = (
        P("grp", SUB, None, None),
        P("grp", SUB, None),
        P("grp", SUB, None, None, None, None),
        P("grp", SUB, None, None),
        P("grp", SUB, None, None),
        P("grp", SUB, None, None),
        P("grp", SUB, None),
    )
    return jax.shard_map(
        per_device, mesh=split, in_specs=specs, out_specs=P("grp", SUB, None, None), check_vma=False
    )
```

time: 278 us -> 200 us (0.72)
  local copies, waits for them, and re-layouts: 52.7 us -> 6.58 us
  blocking collectives: 115 us -> 145 us
  matrix products: 28.2 us -> 0 us
  other arithmetic: 22.7 us -> 1.29 us
  Pallas kernels: 0 us -> 14.4 us
  starting transfers between devices: 42 us -> 27.8 us
  waiting for transfers between devices: 13.2 us -> 2.69 us
    all_to_all x7 -> x8, blocking collectives: 89.6 us -> 124 us  [spread(): return lax.all_to_all(value, axis, 0, 0)]
    dot_general x12 -> x0, matrix products: 28.2 us -> none  [the longest x3 13.3 us: local_part(): jnp.einsum('bkoi,nbki->nbo', blocks, picked, precision=HIGH)]
    reshape x12 -> x0, local copies, waits for them, and re-layouts: 19.4 us -> none  [the longest x6 8.97 us: local_part(): picked = field.reshape(count, nblocks, rows // nblocks)[:, pattern]]
    pallas_call x0 -> x12, Pallas kernels: none -> 14.4 us  [the longest x3 4.02 us: per_device(): call(local_kernel, shape(count, rows), [smem()] + [vmem()] * 3, 20000000,...]
    gather x6 -> x0, local copies, waits for them, and re-layouts: 11.4 us -> none  [the longest x3 5.95 us: local_part(): picked = field.reshape(count, nblocks, rows // nblocks)[:, pattern]]
    ppermute x9, starting transfers between devices: 32 us -> 23.8 us  [the longest x3 11.7 us: per_device(): from_low = lax.ppermute(send_up, 'grp', up)]
    all_to_all x2 -> x1, waiting for transfers between devices: 10.5 us -> 2.67 us  [spread(): return lax.all_to_all(value, axis, 0, 0)]
    scatter-add x3 -> x0, other arithmetic: 6.77 us -> none  [exchange(): zeros.at[:, margin.reshape(-1)].add(received.reshape(count, -1, 128))]
  transfers between devices with their start and end apart: 11 -> 10, of which waited for: 4 -> 1; matrix products, arithmetic and copies ran while one was open for 12% -> 0% of each run, Pallas kernels for 0% -> 4%
where the time goes in v2:
time: 200 us; the launch traced here: 198 us
  blocking collectives  145 us (72%)
  starting transfers between devices  27.8 us (14%)
  Pallas kernels  14.4 us (7%)
  local copies, waits for them, and re-layouts  6.58 us (3%)
  waiting for transfers between devices  2.69 us (1%)
    all_to_all x8, blocking collectives, spread(): return lax.all_to_all(value, axis, 0, 0)  124 us
    all_gather x3, blocking collectives, gather_coarse(): return lax.all_gather(spread(repeated(column, 'x'), 'x'), 'core')  15.7 us
    ppermute x3, starting transfers between devices, per_device(): from_low = lax.ppermute(send_up, 'grp', up)  11.7 us
    ppermute x3, starting transfers between devices, per_device(): other = lax.ppermute(send_across, SUB, across)  8.2 us
    unnamed x18, local copies, waits for them, and re-layouts  5.71 us
    all_gather x3, blocking collectives, per_device(): partner = lax.all_gather(send_partner, 'core')  5.49 us
    pallas_call x3, Pallas kernels, per_device(): call(local_kernel, shape(count, rows), [smem()] + [vmem()] * 3, 20000000,...  4.02 us
    all_to_all x1, starting transfers between devices, spread(): return lax.all_to_all(value, axis, 0, 0)  4.01 us
  transfers between devices with their start and end apart: 10, of which 1 were waited for; matrix products, arithmetic and copies ran while one was open for 0% of the time, Pallas kernels for 4%

profile of v2, /device:TPU:1, one launch (start us, length us, event | category | flops | bytes accessed | tf_op | source)
XLA Modules:
  0.0 197.9 jit_solution(815544382860185679)
XLA Ops:
  3.0 30.8 %all_to_all.45 = f32[16,8,128]{2,1,0:T(8,128)S(1)} all-to-all(f32[16,8,128]{2,1,0:T(8,128)S(1)} %get-tuple-element.28), channel_id=1, replica_groups=mesh['grp'=8,'z'=16,'x'=4,'core'=2] {'z'}, dimensions={0} | all-to-all | bytes 131072 | tf_op jit(solution)/shard_map/all_to_all | solution.py:214
  34.6 4.0 %all-to-all-start.1 = ((f32[4,16,8,128]{3,2,1,0:T(8,128)}), f32[4,16,8,128]{3,2,1,0:T(8,128)S(1)}, u32[]{:S(2)}, u32[]{:S(2)}) async-start(f32[4,16,8,128]{3,2,1,0:T(8,128)} %broadcast_in_dim.12), calls=%async_computation.1 | async-start | bytes 524288 | tf_op jit(solution)/shard_map/all_to_all | solution.py:214
  38.6 1.3 copy-done.1
  39.8 1.6 shard_map.74.coarse_ref
  41.4 2.7 %all-to-all-done.1 = f32[4,16,8,128]{3,2,1,0:T(8,128)S(1)} async-done(((f32[4,16,8,128]{3,2,1,0:T(8,128)}), f32[4,16,8,128]{3,2,1,0:T(8,128)S(1)}, u32[]{:S(2)}, u32[]{:S(2)}) %all-to-all-start.1) | async-done | bytes 262176 | tf_op jit(solution)/shard_map/all_to_all | solution.py:214
  44.1 5.3 %all-gather = f32[8,16,8,128]{3,2,1,0:T(8,128)S(1)} all-gather(f32[4,16,8,128]{3,2,1,0:T(8,128)S(1)} %all-to-all-done.1), channel_id=2, replica_groups=mesh['grp'=8,'z'=16,'x'=4,'core'=2] {'core'}, dimensions={0}, use_global_device_ids=true | all-gather | bytes 786432 | tf_op jit(solution)/shard_map/all_gather | solution.py:223
  50.7 3.2 %collective-permute-start = (f32[8,512]{1,0:T(8,128)S(1)}, f32[8,512]{1,0:T(8,128)S(1)}, u32[]{:S(2)}, u32[]{:S(2)}) collective-permute-start(f32[8,512]{1,0:T(8,128)S(1)} %get-tuple-element.32), channel_id=1, source_target_pairs={{0,128},{128,256},{256,384},{384,512},{512,640},{640,768},{768,896... | collective-permute-start | bytes 49160 | tf_op jit(solution)/shard_map/ppermute | solution.py:344
  53.9 1.3 collective-permute-start.1
  55.2 2.7 %collective-permute-start.2 = (f32[8,512]{1,0:T(8,128)S(1)}, f32[8,512]{1,0:T(8,128)S(1)}, u32[]{:S(2)}, u32[]{:S(2)}) collective-permute-start(f32[8,512]{1,0:T(8,128)S(1)} %get-tuple-element.34), channel_id=1, source_target_pairs={{1,2},{2,1},{3,4},{4,3},{5,6},{6,5},{7,8},{8,7},{9,10},{10,9},{11,... | collective-permute-start | bytes 49160 | tf_op jit(solution)/shard_map/ppermute | solution.py:346
  58.1 1.9 copy-done
  60.0 2.0 shard_map.76.weights_ref
  61.9 1.3 shard_map.77.base_ref
  63.3 1.8 all-gather.1
  66.0 16.4 %all_to_all.46 = f32[16,8,128]{2,1,0:T(8,128)S(1)} all-to-all(f32[16,8,128]{2,1,0:T(8,128)S(1)} %get-tuple-element.37), channel_id=1, replica_groups=mesh['grp'=8,'z'=16,'x'=4,'core'=2] {'z'}, dimensions={0} | all-to-all | bytes 131072 | tf_op jit(solution)/shard_map/all_to_all | solution.py:214
  82.4 8.6 %all_to_all.47 = f32[4,16,8,128]{3,2,1,0:T(8,128)S(1)} all-to-all(f32[4,16,8,128]{3,2,1,0:T(8,128)S(1)} %broadcast_in_dim.13), channel_id=1, replica_groups=mesh['grp'=8,'z'=16,'x'=4,'core'=2] {'x'}, dimensions={0} | all-to-all | bytes 524288 | tf_op jit(solution)/shard_map/all_to_all | solution.py:214
  91.0 5.2 %all-gather.2 = f32[8,16,8,128]{3,2,1,0:T(8,128)S(1)} all-gather(f32[4,16,8,128]{3,2,1,0:T(8,128)S(1)} %all_to_all.47), channel_id=4, replica_groups=mesh['grp'=8,'z'=16,'x'=4,'core'=2] {'core'}, dimensions={0}, use_global_device_ids=true | all-gather | bytes 786432 | tf_op jit(solution)/shard_map/all_gather | solution.py:223
  97.5 4.3 %collective-permute-start.3 = (f32[8,512]{1,0:T(8,128)S(1)}, f32[8,512]{1,0:T(8,128)S(1)}, u32[]{:S(2)}, u32[]{:S(2)}) collective-permute-start(f32[8,512]{1,0:T(8,128)S(1)} %get-tuple-element.40), channel_id=1, source_target_pairs={{0,128},{128,256},{256,384},{384,512},{512,640},{640,768},{768,896... | collective-permute-start | bytes 49160 | tf_op jit(solution)/shard_map/ppermute | solution.py:344
  101.8 1.3 collective-permute-start.4
  103.1 2.7 %collective-permute-start.5 = (f32[8,512]{1,0:T(8,128)S(1)}, f32[8,512]{1,0:T(8,128)S(1)}, u32[]{:S(2)}, u32[]{:S(2)}) collective-permute-start(f32[8,512]{1,0:T(8,128)S(1)} %get-tuple-element.42), channel_id=1, source_target_pairs={{1,2},{2,1},{3,4},{4,3},{5,6},{6,5},{7,8},{8,7},{9,10},{10,9},{11,... | collective-permute-start | bytes 49160 | tf_op jit(solution)/shard_map/ppermute | solution.py:346
  105.8 1.3 shard_map.80.base_ref
  107.1 1.8 all-gather.3
  109.8 16.5 %all_to_all.48 = f32[16,8,128]{2,1,0:T(8,128)S(1)} all-to-all(f32[16,8,128]{2,1,0:T(8,128)S(1)} %get-tuple-element.44), channel_id=1, replica_groups=mesh['grp'=8,'z'=16,'x'=4,'core'=2] {'z'}, dimensions={0} | all-to-all | bytes 131072 | tf_op jit(solution)/shard_map/all_to_all | solution.py:214
  126.3 8.6 %all_to_all.49 = f32[4,16,8,128]{3,2,1,0:T(8,128)S(1)} all-to-all(f32[4,16,8,128]{3,2,1,0:T(8,128)S(1)} %broadcast_in_dim.14), channel_id=1, replica_groups=mesh['grp'=8,'z'=16,'x'=4,'core'=2] {'x'}, dimensions={0} | all-to-all | bytes 524288 | tf_op jit(solution)/shard_map/all_to_all | solution.py:214
  134.9 5.2 %all-gather.4 = f32[8,16,8,128]{3,2,1,0:T(8,128)S(1)} all-gather(f32[4,16,8,128]{3,2,1,0:T(8,128)S(1)} %all_to_all.49), channel_id=6, replica_groups=mesh['grp'=8,'z'=16,'x'=4,'core'=2] {'core'}, dimensions={0}, use_global_device_ids=true | all-gather | bytes 786432 | tf_op jit(solution)/shard_map/all_gather | solution.py:223
  141.4 4.3 %collective-permute-start.6 = (f32[8,512]{1,0:T(8,128)S(1)}, f32[8,512]{1,0:T(8,128)S(1)}, u32[]{:S(2)}, u32[]{:S(2)}) collective-permute-start(f32[8,512]{1,0:T(8,128)S(1)} %get-tuple-element.47), channel_id=1, source_target_pairs={{0,128},{128,256},{256,384},{384,512},{512,640},{640,768},{768,896... | collective-permute-start | bytes 49160 | tf_op jit(solution)/shard_map/ppermute | solution.py:344
  145.7 1.3 collective-permute-start.7
  147.0 2.7 %collective-permute-start.8 = (f32[8,512]{1,0:T(8,128)S(1)}, f32[8,512]{1,0:T(8,128)S(1)}, u32[]{:S(2)}, u32[]{:S(2)}) collective-permute-start(f32[8,512]{1,0:T(8,128)S(1)} %get-tuple-element.49), channel_id=1, source_target_pairs={{1,2},{2,1},{3,4},{4,3},{5,6},{6,5},{7,8},{8,7},{9,10},{10,9},{11,... | collective-permute-start | bytes 49160 | tf_op jit(solution)/shard_map/ppermute | solution.py:346
  149.7 1.3 shard_map.83.base_ref
  151.1 1.8 all-gather.5
  153.7 9.2 %all_to_all.50 = f32[8,8,128]{2,1,0:T(8,128)S(1)} all-to-all(f32[8,8,128]{2,1,0:T(8,128)S(1)} %shard_map.84), channel_id=1, replica_groups=mesh['grp'=8,'z'=16,'x'=4,'core'=2] {'x','core'}, dimensions={0} | all-to-all | bytes 65536 | tf_op jit(solution)/shard_map/all_to_all | solution.py:214
  162.9 15.5 %all_to_all.51 = f32[16,8,128]{2,1,0:T(8,128)S(1)} all-to-all(f32[16,8,128]{2,1,0:T(8,128)S(1)} %broadcast_in_dim.15), channel_id=1, replica_groups=mesh['grp'=8,'z'=16,'x'=4,'core'=2] {'z'}, dimensions={0} | all-to-all | bytes 131072 | tf_op jit(solution)/shard_map/all_to_all | solution.py:214
  178.4 18.2 %all_to_all.52 = f32[8,8,128]{2,1,0:T(8,128)S(1)} all-to-all(f32[8,8,128]{2,1,0:T(8,128)S(1)} %broadcast_in_dim.16), channel_id=1, replica_groups=mesh['grp'=8,'z'=16,'x'=4,'core'=2] {'grp'}, dimensions={0} | all-to-all | bytes 65536 | tf_op jit(solution)/shard_map/all_to_all | solution.py:214
  (44 shorter events, 11.5 us)
Async XLA Ops:
  0.0 0.8 copy-start.2
  0.8 1.0 copy-start.4
  1.8 0.7 copy-start.5
  34.6 9.5 %all-to-all-start.1 = ((f32[4,16,8,128]{3,2,1,0:T(8,128)}), f32[4,16,8,128]{3,2,1,0:T(8,128)S(1)}, u32[]{:S(2)}, u32[]{:S(2)}) async-start(f32[4,16,8,128]{3,2,1,0:T(8,128)} %broadcast_in_dim.12), calls=%async_computation.1 | async-start | bytes 524288 | tf_op jit(solution)/shard_map/all_to_all | solution.py:214
  38.6 1.3 copy-start.1
  39.8 9.6 %copy-start.3 = (f32[1,1,8,2048]{3,2,1,0:T(8,128)S(1)}, f32[1,1,8,2048]{3,2,1,0:T(8,128)}, u32[]{:S(2)}) copy-start(f32[1,1,8,2048]{3,2,1,0:T(8,128)} %param.7) | copy-start | bytes 196612
  39.8 9.6 %copy-start.7 = (s32[1,1,4,4]{3,2,1,0:T(4,128)S(1)}, s32[1,1,4,4]{3,2,1,0:T(4,128)}, u32[]{:S(2)}) copy-start(s32[1,1,4,4]{3,2,1,0:T(4,128)} %param.11) | copy-start | bytes 196
  41.4 16.5 %copy-start.8 = (s32[1,1,32,3]{2,1,3,0:T(1,128)S(1)}, s32[1,1,32,3]{2,1,3,0:T(1,128)}, u32[]{:S(2)}) copy-start(s32[1,1,32,3]{2,1,3,0:T(1,128)} %param.10) | copy-start | bytes 1156
  50.7 14.4 %collective-permute-start = (f32[8,512]{1,0:T(8,128)S(1)}, f32[8,512]{1,0:T(8,128)S(1)}, u32[]{:S(2)}, u32[]{:S(2)}) collective-permute-start(f32[8,512]{1,0:T(8,128)S(1)} %get-tuple-element.32), channel_id=1, source_target_pairs={{0,128},{128,256},{256,384},{384,512},{512,640},{640,768},{768,896... | collective-permute-start | bytes 49160 | tf_op jit(solution)/shard_map/ppermute | solution.py:344
  53.9 11.2 %collective-permute-start.1 = (f32[8,512]{1,0:T(8,128)S(1)}, f32[8,512]{1,0:T(8,128)S(1)}, u32[]{:S(2)}, u32[]{:S(2)}) collective-permute-start(f32[8,512]{1,0:T(8,128)S(1)} %get-tuple-element.33), channel_id=1, source_target_pairs={{128,0},{256,128},{384,256},{512,384},{640,512},{768,640},{896,768... | collective-permute-start | bytes 49160 | tf_op jit(solution)/shard_map/ppermute | solution.py:345
  55.2 9.9 %collective-permute-start.2 = (f32[8,512]{1,0:T(8,128)S(1)}, f32[8,512]{1,0:T(8,128)S(1)}, u32[]{:S(2)}, u32[]{:S(2)}) collective-permute-start(f32[8,512]{1,0:T(8,128)S(1)} %get-tuple-element.34), channel_id=1, source_target_pairs={{1,2},{2,1},{3,4},{4,3},{5,6},{6,5},{7,8},{8,7},{9,10},{10,9},{11,... | collective-permute-start | bytes 49160 | tf_op jit(solution)/shard_map/ppermute | solution.py:346
  58.1 1.9 copy-start
  60.0 2.0 copy-start.6
  97.5 11.5 %collective-permute-start.3 = (f32[8,512]{1,0:T(8,128)S(1)}, f32[8,512]{1,0:T(8,128)S(1)}, u32[]{:S(2)}, u32[]{:S(2)}) collective-permute-start(f32[8,512]{1,0:T(8,128)S(1)} %get-tuple-element.40), channel_id=1, source_target_pairs={{0,128},{128,256},{256,384},{384,512},{512,640},{640,768},{768,896... | collective-permute-start | bytes 49160 | tf_op jit(solution)/shard_map/ppermute | solution.py:344
  101.8 7.2 %collective-permute-start.4 = (f32[8,512]{1,0:T(8,128)S(1)}, f32[8,512]{1,0:T(8,128)S(1)}, u32[]{:S(2)}, u32[]{:S(2)}) collective-permute-start(f32[8,512]{1,0:T(8,128)S(1)} %get-tuple-element.41), channel_id=1, source_target_pairs={{128,0},{256,128},{384,256},{512,384},{640,512},{768,640},{896,768... | collective-permute-start | bytes 49160 | tf_op jit(solution)/shard_map/ppermute | solution.py:345
  103.1 5.9 %collective-permute-start.5 = (f32[8,512]{1,0:T(8,128)S(1)}, f32[8,512]{1,0:T(8,128)S(1)}, u32[]{:S(2)}, u32[]{:S(2)}) collective-permute-start(f32[8,512]{1,0:T(8,128)S(1)} %get-tuple-element.42), channel_id=1, source_target_pairs={{1,2},{2,1},{3,4},{4,3},{5,6},{6,5},{7,8},{8,7},{9,10},{10,9},{11,... | collective-permute-start | bytes 49160 | tf_op jit(solution)/shard_map/ppermute | solution.py:346
  141.4 11.5 %collective-permute-start.6 = (f32[8,512]{1,0:T(8,128)S(1)}, f32[8,512]{1,0:T(8,128)S(1)}, u32[]{:S(2)}, u32[]{:S(2)}) collective-permute-start(f32[8,512]{1,0:T(8,128)S(1)} %get-tuple-element.47), channel_id=1, source_target_pairs={{0,128},{128,256},{256,384},{384,512},{512,640},{640,768},{768,896... | collective-permute-start | bytes 49160 | tf_op jit(solution)/shard_map/ppermute | solution.py:344
  145.7 7.2 %collective-permute-start.7 = (f32[8,512]{1,0:T(8,128)S(1)}, f32[8,512]{1,0:T(8,128)S(1)}, u32[]{:S(2)}, u32[]{:S(2)}) collective-permute-start(f32[8,512]{1,0:T(8,128)S(1)} %get-tuple-element.48), channel_id=1, source_target_pairs={{128,0},{256,128},{384,256},{512,384},{640,512},{768,640},{896,768... | collective-permute-start | bytes 49160 | tf_op jit(solution)/shard_map/ppermute | solution.py:345
  147.0 5.9 %collective-permute-start.8 = (f32[8,512]{1,0:T(8,128)S(1)}, f32[8,512]{1,0:T(8,128)S(1)}, u32[]{:S(2)}, u32[]{:S(2)}) collective-permute-start(f32[8,512]{1,0:T(8,128)S(1)} %get-tuple-element.49), channel_id=1, source_target_pairs={{1,2},{2,1},{3,4},{4,3},{5,6},{6,5},{7,8},{8,7},{9,10},{10,9},{11,... | collective-permute-start | bytes 49160 | tf_op jit(solution)/shard_map/ppermute | solution.py:346

commit v3 on v2

--- a/solution.py
+++ b/solution.py
@@ -24,14 +24,14 @@
     return pl.BlockSpec(memory_space=pltpu.SMEM)
 
 
-def call(body, outs, specs, flops, nbytes, scratch=()):
+def call(body, outs, specs, flops, nbytes, scratch=(), grant=16):
     return pl.pallas_call(
         body,
         out_shape=outs,
         in_specs=specs,
         out_specs=jax.tree.map(lambda _: vmem(), outs),
         scratch_shapes=scratch,
-        compiler_params=pltpu.CompilerParams(vmem_limit_bytes=40 * 1024 * 1024),
+        compiler_params=pltpu.CompilerParams(vmem_limit_bytes=grant * 1024 * 1024),
         cost_estimate=pl.CostEstimate(flops=flops, bytes_accessed=nbytes, transcendentals=0),
     )
 
@@ -50,14 +50,17 @@
     return lax.broadcasted_iota(jnp.int32, shape, len(shape) - 1)
 
 
-def coarse_piece(field, basis_t, core):
+def coarse_piece(field, basis_t, core, gen):
     count = field.shape[0]
     out = jnp.dot(stacked(field), basis_t, preferred_element_type=F32)
     lane = lane_of((count, LANES))
     part = out[:count] + jnp.where(lane < HALF, out[count:], 0.0)
     both = part + pltpu.roll(part, HALF, 1)
-    start = core * HALF
-    return jnp.where((lane >= start) & (lane < start + 48), both, 0.0)
+    half = count // 2
+    lane = lane_of((half, LANES))
+    own = (lane < HALF) == (core == 0)
+    piece = jnp.where(own, both[:half], both[half:])
+    return jnp.where((lane & (HALF - 1)) < gen, piece, 0.0)
 
 
 def transposed_halves(value):
@@ -70,18 +73,32 @@
     return jnp.concatenate(parts, axis=0).T.astype(BF16)
 
 
-def start_kernel(core_ref, rhs_ref, basis_ref, diag_ref, basis_t_ref, basis_h_ref, inv_ref, piece_ref):
-    rows = basis_ref.shape[1]
+def start_kernel(
+    core_ref, rhs_hbm, basis_hbm, diag_hbm, basis_t_ref, basis_h_ref, inv_ref, piece_ref,
+    rhs_ref, basis_ref, diag_ref, sems,
+):
+    copies = [
+        pltpu.make_async_copy(source, target, sems.at[i])
+        for i, (source, target) in enumerate(
+            ((basis_hbm, basis_ref), (rhs_hbm, rhs_ref), (diag_hbm, diag_ref))
+        )
+    ]
+    for copy in copies:
+        copy.start()
+    gen, rows = basis_ref.shape
+    copies[0].wait()
     for t in range(rows // LANES):
         cols = slice(t * LANES, (t + 1) * LANES)
         basis_t_ref[cols, :] = transposed_halves(basis_ref[:, cols])
+    copies[1].wait()
+    piece = coarse_piece(rhs_ref[...], basis_t_ref[...], core_ref[0], gen)
+    for t in range(piece_ref.shape[0]):
+        piece_ref[t] = piece
     high, low = halves(basis_ref[...])
     basis_h_ref[:, :rows] = high.astype(BF16)
     basis_h_ref[:, rows:] = low.astype(BF16)
+    copies[2].wait()
     inv_ref[...] = 1.0 / diag_ref[...]
-    piece = coarse_piece(rhs_ref[...], basis_t_ref[...], core_ref[0])
-    for z in range(piece_ref.shape[0]):
-        piece_ref[z] = piece
 
 
 def coarse_kernel(inverse_ref, out_ref):
@@ -115,22 +132,32 @@
     lax.fori_loop(0, nblocks // 2, step, 0)
 
 
+def prepare_kernel(inverse_ref, blocks_ref, coarse_ref, weights_ref):
+    coarse_kernel(inverse_ref, coarse_ref)
+    block_kernel(blocks_ref, weights_ref)
+
+
 def field_kernel(
     core_ref, margin_ref, pieces_ref, k_ref, inv_ref, coarse_ref, basis_h_ref,
     p_ref, up_ref, down_ref, across_ref, partner_ref, packed_ref,
 ):
     count, rows = k_ref.shape
-    _, xs, zs, _, _ = pieces_ref.shape
-    for z in range(zs):
-        for x in range(xs):
-            t = z * xs + x
-            packed_ref[:, t * LANES : (t + 1) * LANES] = stacked(
-                pieces_ref[0, x, z] + pieces_ref[1, x, z]
-            )
+    gen = basis_h_ref.shape[0]
+    lower = lane_of((count // 2, LANES)) < HALF
+    for t in range(pieces_ref.shape[1]):
+        first, second = pieces_ref[0, t], pieces_ref[1, t]
+        tile = jnp.concatenate(
+            [
+                jnp.where(lower, first, second),
+                pltpu.roll(jnp.where(lower, second, first), HALF, 1),
+            ],
+            axis=0,
+        )
+        packed_ref[:, t * LANES : (t + 1) * LANES] = stacked(tile)
     out = jnp.dot(packed_ref[...], coarse_ref[...], preferred_element_type=F32)
     part = out[:count] + jnp.where(lane_of((count, LANES)) < HALF, out[count:], 0.0)
     answer = part + pltpu.roll(part, HALF, 1)
-    back = jnp.dot(stacked(answer[:, :48]), basis_h_ref[...], preferred_element_type=F32)
+    back = jnp.dot(stacked(answer[:, :gen]), basis_h_ref[...], preferred_element_type=F32)
     p_ref[...] = (
         k_ref[...] * inv_ref[...] + (back[:count, :rows] + back[count:, :rows]) + back[:count, rows:]
     )
@@ -172,10 +199,10 @@
         out_ref[:, cols] = diag_ref[:, cols] * p_ref[:, cols] + local
 
 
-def couple(core_ref, margin_ref, base_ref, low_ref, high_ref, across_ref, both_ref, k_ref):
+def couple(core_ref, margin_ref, base_ref, low_ref, high_ref, across_ref, partner_ref, k_ref):
     core = core_ref[0]
     k_ref[...] = base_ref[...]
-    for d, source in ((0, low_ref), (1, high_ref), (2 + core, across_ref), (3 - core, both_ref.at[1 - core])):
+    for d, source in ((0, low_ref), (1, high_ref), (2 + core, across_ref), (3 - core, partner_ref)):
         for j in range(margin_ref.shape[1]):
             at = pl.ds(pl.multiple_of(margin_ref[d, j] * LANES, LANES), LANES)
             k_ref[:, at] = k_ref[:, at] - source[:, j * LANES : (j + 1) * LANES]
@@ -183,30 +210,45 @@
 
 
 def next_kernel(
-    core_ref, margin_ref, base_ref, low_ref, high_ref, across_ref, both_ref, basis_t_ref,
+    gen, core_ref, margin_ref, base_ref, low_ref, high_ref, across_ref, partner_ref, basis_t_ref,
     k_ref, piece_ref,
 ):
-    couple(core_ref, margin_ref, base_ref, low_ref, high_ref, across_ref, both_ref, k_ref)
-    piece = coarse_piece(k_ref[...], basis_t_ref[...], core_ref[0])
-    for z in range(piece_ref.shape[0]):
-        piece_ref[z] = piece
+    couple(core_ref, margin_ref, base_ref, low_ref, high_ref, across_ref, partner_ref, k_ref)
+    piece = coarse_piece(k_ref[...], basis_t_ref[...], core_ref[0], gen)
+    for t in range(piece_ref.shape[0]):
+        piece_ref[t] = piece
 
 
 def gram_kernel(
-    core_ref, margin_ref, base_ref, low_ref, high_ref, across_ref, both_ref, k0_ref, k1_ref, k2_ref,
+    core_ref, margin_ref, base_ref, low_ref, high_ref, across_ref, partner_ref, k0_ref, k1_ref, k2_ref,
     sums_ref, k3_ref,
 ):
-    couple(core_ref, margin_ref, base_ref, low_ref, high_ref, across_ref, both_ref, k3_ref)
+    couple(core_ref, margin_ref, base_ref, low_ref, high_ref, across_ref, partner_ref, k3_ref)
     fields = [k0_ref[...], k1_ref[...], k2_ref[...], k3_ref[...]]
     count = fields[0].shape[0]
     lane = lane_of((count, LANES))
+    place = lane - SLOTS * lax.broadcasted_iota(jnp.int32, (count, LANES), 0)
     sums = jnp.zeros((count, LANES), F32)
     for at, (i, j) in enumerate(PAIRS):
-        sums = jnp.where(lane == at, jnp.sum(fields[i] * fields[j], axis=1, keepdims=True), sums)
+        sums = jnp.where(place == at, jnp.sum(fields[i] * fields[j], axis=1, keepdims=True), sums)
+    sums = jnp.sum(sums, axis=0, keepdims=True)
     for n in range(sums_ref.shape[0]):
         sums_ref[n] = sums
 
 
+def finish_kernel(sums_ref, p0_ref, p1_ref, p2_ref, out_ref):
+    count = p0_ref.shape[0]
+    sums = jnp.broadcast_to(jnp.sum(sums_ref[...], axis=0), (count, LANES))
+    row = lax.broadcasted_iota(jnp.int32, (count, LANES), 0)
+    place = lane_of((count, LANES)) - SLOTS * row
+    gram = [[None] * (ITERS + 1) for _ in range(ITERS + 1)]
+    for at, (i, j) in enumerate(PAIRS):
+        gram[i][j] = jnp.sum(jnp.where(place == at, sums, 0.0), axis=1, keepdims=True)
+    first, second, third = combine(gram)
+    out_ref[...] = first * p0_ref[...] + second * p1_ref[...] + third * p2_ref[...]
+
+
+SLOTS = 16
 PAIRS = [(i, j) for j in range(ITERS + 1) for i in range(j + 1)]
 
 
@@ -218,15 +260,9 @@
     return jnp.broadcast_to(value[None], (lax.axis_size(axis),) + value.shape)
 
 
-def gather_coarse(piece):
-    column = spread(piece, "z")
-    return lax.all_gather(spread(repeated(column, "x"), "x"), "core")
-
-
 def total(values):
-    part = jnp.sum(spread(values, ("x", "core")), axis=0)
-    part = jnp.sum(spread(repeated(part, "z"), "z"), axis=0)
-    return jnp.sum(spread(repeated(part, "grp"), "grp"), axis=0)
+    part = jnp.sum(spread(values, ("z", "x")), axis=0)
+    return spread(repeated(part, ("grp", "core")), ("grp", "core"))
 
 
 def least_squares(columns, beta):
@@ -315,23 +351,44 @@
     across = [(i, ((i + 1) ^ 1) - 1) for i in range(1, subs - 1)]
     wide = subs * HALF
 
+    chips = zs * xs
+    anywhere = pl.BlockSpec(memory_space=pl.ANY)
+
     basis_t, basis_h, inv_row, piece = call(
         start_kernel,
-        [shape(rows, LANES, dtype=BF16), shape(gen, 2 * rows, dtype=BF16), shape(1, rows), shape(zs, count, LANES)],
-        [smem(), vmem(), vmem(), vmem()],
+        [
+            shape(rows, LANES, dtype=BF16),
+            shape(gen, 2 * rows, dtype=BF16),
+            shape(1, rows),
+            shape(chips, count // 2, LANES),
+        ],
+        [smem(), anywhere, anywhere, anywhere],
         3_000_000,
         1_500_000,
+        [
+            pltpu.VMEM((count, rows), F32),
+            pltpu.VMEM((gen, rows), F32),
+            pltpu.VMEM((1, rows), F32),
+            pltpu.SemaphoreType.DMA((3,)),
+        ],
+        60,
     )(core, source, basis, diag_row)
-    coarse = call(coarse_kernel, shape(wide, LANES, dtype=BF16), [vmem()], 1_000_000, 3_200_000)(inverse)
-    weights = call(
-        block_kernel, shape(nblocks, 4 * HALF, LANES, dtype=BF16), [vmem()], 1_000_000, 5_000_000
-    )(blocks[0, 0])
+    coarse, weights = call(
+        prepare_kernel,
+        [shape(wide, LANES, dtype=BF16), shape(nblocks, 4 * HALF, LANES, dtype=BF16)],
+        [vmem(), vmem()],
+        2_000_000,
+        8_000_000,
+    )(inverse, blocks[0, 0])
 
     krylov = [source]
     conditioned = []
     sums = None
     for step in range(ITERS):
-        pieces = gather_coarse(piece)
+        pieces = spread(piece, ("z", "x"))
+        if step == 0:
+            pieces, coarse, weights = lax.optimization_barrier((pieces, coarse, weights))
+        pieces = lax.all_gather(pieces, "core")
         p, send_up, send_down, send_across, send_partner = call(
             field_kernel,
             [shape(count, rows)] + [shape(count, rim)] * 4,
@@ -344,7 +401,7 @@
         from_low = lax.ppermute(send_up, "grp", up)
         from_high = lax.ppermute(send_down, "grp", down)
         other = lax.ppermute(send_across, SUB, across)
-        partner = lax.all_gather(send_partner, "core")
+        partner = lax.ppermute(send_partner, "core", [(0, 1), (1, 0)])
         base = call(
             local_kernel,
             shape(count, rows),
@@ -356,8 +413,8 @@
         shared = (core, margin, base, from_low, from_high, other, partner)
         if step < ITERS - 1:
             field, piece = call(
-                next_kernel,
-                [shape(count, rows), shape(zs, count, LANES)],
+                functools.partial(next_kernel, gen),
+                [shape(count, rows), shape(chips, count // 2, LANES)],
                 [smem(), smem()] + [vmem()] * 6,
                 4_000_000,
                 1_000_000,
@@ -366,18 +423,15 @@
         else:
             sums = call(
                 gram_kernel,
-                shape(2 * xs, count, LANES),
+                shape(chips, 1, LANES),
                 [smem(), smem()] + [vmem()] * 8,
                 400_000,
                 500_000,
                 [pltpu.VMEM((count, rows), F32)],
             )(*shared, *krylov)
-    sums = total(sums)
-    gram = [[None] * (ITERS + 1) for _ in range(ITERS + 1)]
-    for at, (i, j) in enumerate(PAIRS):
-        gram[i][j] = sums[:, at : at + 1]
-    factors = combine(gram)
-    result = sum(f * p for f, p in zip(factors, conditioned))
+    result = call(finish_kernel, shape(count, rows), [vmem()] * 4, 100_000, 300_000)(
+        total(sums), *conditioned
+    )
     return result[None, None]
 
 

time: 200 us -> 185 us (0.925)
  blocking collectives: 145 us -> 101 us
  starting transfers between devices: 27.8 us -> 52.1 us
  waiting for transfers between devices: 2.69 us -> 6.88 us
  Pallas kernels: 14.4 us -> 17.4 us
    all_to_all x8 -> x4, blocking collectives: 124 us -> 85.4 us  [spread(): return lax.all_to_all(value, axis, 0, 0)]
    all_to_all x1, starting transfers between devices: 4.01 us -> 22.8 us  [spread(): return lax.all_to_all(value, axis, 0, 0)]
    ppermute x0 -> x3, starting transfers between devices: none -> 5.76 us  [per_device(): partner = lax.ppermute(send_partner, 'core', [(0, 1), (1, 0)])]
    all_gather x6 -> x3, blocking collectives: 21.2 us -> 15.7 us  [per_device(): pieces = lax.all_gather(pieces, 'core')]
    all_to_all x1, waiting for transfers between devices: 2.67 us -> 6.83 us  [spread(): return lax.all_to_all(value, axis, 0, 0)]
    pallas_call x1, Pallas kernels: 0.51 us -> 2.56 us  [per_device(): call(start_kernel, [shape(rows, LANES, dtype=BF16), shape(gen, 2 * rows,...]
    unnamed x18 -> x24, local copies, waits for them, and re-layouts: 5.71 us -> 6.11 us
  transfers between devices with their start and end apart: 10 -> 13, of which waited for: 1 -> 1; matrix products, arithmetic and copies ran while one was open for 0% -> 0% of each run, Pallas kernels for 4% -> 4%
where the time goes in v3:
time: 185 us; the launch traced here: 184 us
  blocking collectives  101 us (55%)
  starting transfers between devices  52.1 us (28%)
  Pallas kernels  17.4 us (9%)
  waiting for transfers between devices  6.88 us (4%)
  local copies, waits for them, and re-layouts  6.21 us (3%)
    all_to_all x4, blocking collectives, spread(): return lax.all_to_all(value, axis, 0, 0)  85.4 us
    all_to_all x1, starting transfers between devices, spread(): return lax.all_to_all(value, axis, 0, 0)  22.8 us
    all_gather x3, blocking collectives, per_device(): pieces = lax.all_gather(pieces, 'core')  15.7 us
    ppermute x3, starting transfers between devices, per_device(): from_low = lax.ppermute(send_up, 'grp', up)  11.7 us
    ppermute x3, starting transfers between devices, per_device(): other = lax.ppermute(send_across, SUB, across)  7.93 us
    all_to_all x1, waiting for transfers between devices, spread(): return lax.all_to_all(value, axis, 0, 0)  6.83 us
    unnamed x24, local copies, waits for them, and re-layouts  6.11 us
    ppermute x3, starting transfers between devices, per_device(): partner = lax.ppermute(send_partner, 'core', [(0, 1), (1, 0)])  5.76 us
  transfers between devices with their start and end apart: 13, of which 1 were waited for; matrix products, arithmetic and copies ran while one was open for 0% of the time, Pallas kernels for 4%

profile of v3, /device:TPU:1, one launch (start us, length us, event | category | flops | bytes accessed | tf_op | source)
XLA Modules:
  0.0 184.0 jit_solution(10928358197523515136)
XLA Ops:
  0.0 2.6 %shard_map.73 = (bf16[2048,128]{1,0:T(8,128)(2,1)}, bf16[48,4096]{1,0:T(8,128)(2,1)}, f32[1,2048]{1,0:T(1,128)}, f32[64,4,128]{2,1,0:T(4,128)}) custom-call(s32[1]{0:T(128)} %bitcast.core_ref, f32[8,2048]{1,0:T(8,128)} %bitcast.17, f32[48,2048]{1,0:T(8,128)} %bitcast.33, f32[1,2048]{1,0:T(1,128)} %bitcast.23), custom_call_target="tpu_custom_call" | custom-call | flops 3000000 | bytes 1500000 | tf_op jit(solution)/shard_map/pallas_call | solution.py:357
  2.6 22.8 %all-to-all-start = ((f32[64,4,128]{2,1,0:T(4,128)}), f32[64,4,128]{2,1,0:T(4,128)S(1)}, u32[]{:S(2)}, u32[]{:S(2)}) async-start(f32[64,4,128]{2,1,0:T(4,128)} %get-tuple-element.33), calls=%async_computation | async-start | bytes 262144 | tf_op jit(solution)/shard_map/all_to_all | solution.py:256
  25.4 1.9 %copy-done.4 = f32[1,1,32,3,64,64]{5,4,3,2,1,0:T(8,128)S(1)} copy-done((f32[1,1,32,3,64,64]{5,4,3,2,1,0:T(8,128)S(1)}, f32[1,1,32,3,64,64]{5,4,3,2,1,0:T(8,128)}, u32[]{:S(2)}) %copy-start.4) | copy-done | bytes 1572888
  28.5 3.5 %shard_map.74 = (bf16[8192,128]{1,0:T(8,128)(2,1)S(1)}, bf16[32,256,128]{2,1,0:T(8,128)(2,1)S(1)}) custom-call(f32[48,6144]{1,0:T(8,128)S(1)} %bitcast.13, f32[32,3,64,64]{3,2,1,0:T(8,128)S(1)} %bitcast.12), custom_call_target="tpu_custom_call" | custom-call | flops 2000000 | bytes 8000000 | tf_op jit(solution)/shard_map/pallas_call | solution.py:376
  32.1 1.3 copy-done
  33.4 6.8 %all-to-all-done = f32[64,4,128]{2,1,0:T(4,128)S(1)} async-done(((f32[64,4,128]{2,1,0:T(4,128)}), f32[64,4,128]{2,1,0:T(4,128)S(1)}, u32[]{:S(2)}, u32[]{:S(2)}) %all-to-all-start) | async-done | bytes 131104 | tf_op jit(solution)/shard_map/all_to_all | solution.py:256
  40.3 5.4 %all-gather = f32[128,4,128]{2,1,0:T(4,128)S(1)} all-gather(f32[64,4,128]{2,1,0:T(4,128)S(1)} %all-to-all-done), channel_id=2, replica_groups=mesh['grp'=8,'z'=16,'x'=4,'core'=2] {'core'}, dimensions={0}, use_global_device_ids=true | all-gather | bytes 393216 | tf_op jit(solution)/shard_map/all_gather | solution.py:391
  45.6 1.6 copy-done.1
  47.2 1.3 shard_map.75
  48.5 3.2 %collective-permute-start = (f32[8,512]{1,0:T(8,128)S(1)}, f32[8,512]{1,0:T(8,128)S(1)}, u32[]{:S(2)}, u32[]{:S(2)}) collective-permute-start(f32[8,512]{1,0:T(8,128)S(1)} %get-tuple-element.42), channel_id=1, source_target_pairs={{0,128},{128,256},{256,384},{384,512},{512,640},{640,768},{768,896... | collective-permute-start | bytes 49160 | tf_op jit(solution)/shard_map/ppermute | solution.py:401
  51.7 1.3 collective-permute-start.1
  53.0 2.6 %collective-permute-start.2 = (f32[8,512]{1,0:T(8,128)S(1)}, f32[8,512]{1,0:T(8,128)S(1)}, u32[]{:S(2)}, u32[]{:S(2)}) collective-permute-start(f32[8,512]{1,0:T(8,128)S(1)} %get-tuple-element.44), channel_id=1, source_target_pairs={{1,2},{2,1},{3,4},{4,3},{5,6},{6,5},{7,8},{8,7},{9,10},{10,9},{11,... | collective-permute-start | bytes 49160 | tf_op jit(solution)/shard_map/ppermute | solution.py:403
  55.7 1.9 %collective-permute-start.3 = (f32[8,512]{1,0:T(8,128)S(1)}, f32[8,512]{1,0:T(8,128)S(1)}, u32[]{:S(2)}, u32[]{:S(2)}) collective-permute-start(f32[8,512]{1,0:T(8,128)S(1)} %get-tuple-element.45), channel_id=1, source_target_pairs={{0,1},{1,0},{2,3},{3,2},{4,5},{5,4},{6,7},{7,6},{8,9},{9,8},{10,11... | collective-permute-start | bytes 49160 | tf_op jit(solution)/shard_map/ppermute | solution.py:404
  57.7 1.3 shard_map.76.base_ref
  60.0 22.2 %all_to_all.25 = f32[64,4,128]{2,1,0:T(4,128)S(1)} all-to-all(f32[64,4,128]{2,1,0:T(4,128)S(1)} %get-tuple-element.47), channel_id=1, replica_groups=mesh['grp'=8,'z'=16,'x'=4,'core'=2] {'z','x'}, dimensions={0} | all-to-all | bytes 262144 | tf_op jit(solution)/shard_map/all_to_all | solution.py:256
  82.2 5.2 %all-gather.1 = f32[128,4,128]{2,1,0:T(4,128)S(1)} all-gather(f32[64,4,128]{2,1,0:T(4,128)S(1)} %all_to_all.25), channel_id=3, replica_groups=mesh['grp'=8,'z'=16,'x'=4,'core'=2] {'core'}, dimensions={0}, use_global_device_ids=true | all-gather | bytes 393216 | tf_op jit(solution)/shard_map/all_gather | solution.py:391
  87.3 1.3 shard_map.78
  88.6 4.3 %collective-permute-start.4 = (f32[8,512]{1,0:T(8,128)S(1)}, f32[8,512]{1,0:T(8,128)S(1)}, u32[]{:S(2)}, u32[]{:S(2)}) collective-permute-start(f32[8,512]{1,0:T(8,128)S(1)} %get-tuple-element.50), channel_id=1, source_target_pairs={{0,128},{128,256},{256,384},{384,512},{512,640},{640,768},{768,896... | collective-permute-start | bytes 49160 | tf_op jit(solution)/shard_map/ppermute | solution.py:401
  92.9 1.3 collective-permute-start.5
  94.2 2.7 %collective-permute-start.6 = (f32[8,512]{1,0:T(8,128)S(1)}, f32[8,512]{1,0:T(8,128)S(1)}, u32[]{:S(2)}, u32[]{:S(2)}) collective-permute-start(f32[8,512]{1,0:T(8,128)S(1)} %get-tuple-element.52), channel_id=1, source_target_pairs={{1,2},{2,1},{3,4},{4,3},{5,6},{6,5},{7,8},{8,7},{9,10},{10,9},{11,... | collective-permute-start | bytes 49160 | tf_op jit(solution)/shard_map/ppermute | solution.py:403
  96.9 1.9 %collective-permute-start.7 = (f32[8,512]{1,0:T(8,128)S(1)}, f32[8,512]{1,0:T(8,128)S(1)}, u32[]{:S(2)}, u32[]{:S(2)}) collective-permute-start(f32[8,512]{1,0:T(8,128)S(1)} %get-tuple-element.53), channel_id=1, source_target_pairs={{0,1},{1,0},{2,3},{3,2},{4,5},{5,4},{6,7},{7,6},{8,9},{9,8},{10,11... | collective-permute-start | bytes 49160 | tf_op jit(solution)/shard_map/ppermute | solution.py:404
  98.8 1.3 shard_map.79.base_ref
  101.1 22.2 %all_to_all.26 = f32[64,4,128]{2,1,0:T(4,128)S(1)} all-to-all(f32[64,4,128]{2,1,0:T(4,128)S(1)} %get-tuple-element.54), channel_id=1, replica_groups=mesh['grp'=8,'z'=16,'x'=4,'core'=2] {'z','x'}, dimensions={0} | all-to-all | bytes 262144 | tf_op jit(solution)/shard_map/all_to_all | solution.py:256
  123.2 5.2 %all-gather.2 = f32[128,4,128]{2,1,0:T(4,128)S(1)} all-gather(f32[64,4,128]{2,1,0:T(4,128)S(1)} %all_to_all.26), channel_id=4, replica_groups=mesh['grp'=8,'z'=16,'x'=4,'core'=2] {'core'}, dimensions={0}, use_global_device_ids=true | all-gather | bytes 393216 | tf_op jit(solution)/shard_map/all_gather | solution.py:391
  128.4 1.3 shard_map.81
  129.7 4.3 %collective-permute-start.8 = (f32[8,512]{1,0:T(8,128)S(1)}, f32[8,512]{1,0:T(8,128)S(1)}, u32[]{:S(2)}, u32[]{:S(2)}) collective-permute-start(f32[8,512]{1,0:T(8,128)S(1)} %get-tuple-element.57), channel_id=1, source_target_pairs={{0,128},{128,256},{256,384},{384,512},{512,640},{640,768},{768,896... | collective-permute-start | bytes 49160 | tf_op jit(solution)/shard_map/ppermute | solution.py:401
  133.9 1.3 collective-permute-start.9
  135.2 2.7 %collective-permute-start.10 = (f32[8,512]{1,0:T(8,128)S(1)}, f32[8,512]{1,0:T(8,128)S(1)}, u32[]{:S(2)}, u32[]{:S(2)}) collective-permute-start(f32[8,512]{1,0:T(8,128)S(1)} %get-tuple-element.59), channel_id=1, source_target_pairs={{1,2},{2,1},{3,4},{4,3},{5,6},{6,5},{7,8},{8,7},{9,10},{10,9},{11,... | collective-permute-start | bytes 49160 | tf_op jit(solution)/shard_map/ppermute | solution.py:403
  137.9 1.9 %collective-permute-start.11 = (f32[8,512]{1,0:T(8,128)S(1)}, f32[8,512]{1,0:T(8,128)S(1)}, u32[]{:S(2)}, u32[]{:S(2)}) collective-permute-start(f32[8,512]{1,0:T(8,128)S(1)} %get-tuple-element.60), channel_id=1, source_target_pairs={{0,1},{1,0},{2,3},{3,2},{4,5},{5,4},{6,7},{7,6},{8,9},{9,8},{10,11... | collective-permute-start | bytes 49160 | tf_op jit(solution)/shard_map/ppermute | solution.py:404
  139.8 1.3 shard_map.82.base_ref
  142.0 20.5 %all_to_all.27 = f32[64,1,128]{2,1,0:T(1,128)S(1)} all-to-all(f32[64,1,128]{2,1,0:T(1,128)S(1)} %shard_map.83), channel_id=1, replica_groups=mesh['grp'=8,'z'=16,'x'=4,'core'=2] {'z','x'}, dimensions={0} | all-to-all | bytes 65536 | tf_op jit(solution)/shard_map/all_to_all | solution.py:256
  162.6 20.5 %all_to_all.28.sums_ref = f32[16,1,128]{2,1,0:T(1,128)S(1)} all-to-all(f32[16,1,128]{2,1,0:T(1,128)S(1)} %broadcast_in_dim.4), channel_id=1, replica_groups=mesh['grp'=8,'z'=16,'x'=4,'core'=2] {'grp','core'}, dimensions={0} | all-to-all | bytes 16384 | tf_op jit(solution)/shard_map/all_to_all | solution.py:256
  (40 shorter events, 5.0 us)
Async XLA Ops:
  2.6 37.7 %all-to-all-start = ((f32[64,4,128]{2,1,0:T(4,128)}), f32[64,4,128]{2,1,0:T(4,128)S(1)}, u32[]{:S(2)}, u32[]{:S(2)}) async-start(f32[64,4,128]{2,1,0:T(4,128)} %get-tuple-element.33), calls=%async_computation | async-start | bytes 262144 | tf_op jit(solution)/shard_map/all_to_all | solution.py:256
  25.4 1.9 %copy-start.4 = (f32[1,1,32,3,64,64]{5,4,3,2,1,0:T(8,128)S(1)}, f32[1,1,32,3,64,64]{5,4,3,2,1,0:T(8,128)}, u32[]{:S(2)}) copy-start(f32[1,1,32,3,64,64]{5,4,3,2,1,0:T(8,128)} %param.9) | copy-start | bytes 4718596
  27.3 1.3 copy-start.6
  28.5 17.1 %copy-start.3 = (bf16[48,4096]{1,0:T(8,128)(2,1)S(1)}, bf16[48,4096]{1,0:T(8,128)(2,1)}, u32[]{:S(2)}) copy-start(bf16[48,4096]{1,0:T(8,128)(2,1)} %get-tuple-element.39.basis_h_ref) | copy-start | bytes 1179652
  28.5 17.1 %copy-start.7 = (f32[1,1,8,2048]{3,2,1,0:T(8,128)S(1)}, f32[1,1,8,2048]{3,2,1,0:T(8,128)}, u32[]{:S(2)}) copy-start(f32[1,1,8,2048]{3,2,1,0:T(8,128)} %param.7) | copy-start | bytes 196612
  28.5 17.1 %copy-start.9 = (f32[1,2048]{1,0:T(1,128)S(1)}, f32[1,2048]{1,0:T(1,128)}, u32[]{:S(2)}) copy-start(f32[1,2048]{1,0:T(1,128)} %get-tuple-element.37.inv_ref) | copy-start | bytes 24580
  28.5 17.1 %copy-start.10 = (s32[1,1,4,4]{3,2,1,0:T(4,128)S(1)}, s32[1,1,4,4]{3,2,1,0:T(4,128)}, u32[]{:S(2)}) copy-start(s32[1,1,4,4]{3,2,1,0:T(4,128)} %param.11) | copy-start | bytes 196
  32.1 1.4 copy-start
  33.4 24.2 %copy-start.11 = (s32[1,1,32,3]{2,1,3,0:T(1,128)S(1)}, s32[1,1,32,3]{2,1,3,0:T(1,128)}, u32[]{:S(2)}) copy-start(s32[1,1,32,3]{2,1,3,0:T(1,128)} %param.10) | copy-start | bytes 1156
  33.4 24.3 %copy-start.8 = (f32[1,1,2048]{2,1,0:T(1,128)S(1)}, f32[1,1,2048]{2,1,0:T(1,128)}, u32[]{:S(2)}) copy-start(f32[1,1,2048]{2,1,0:T(1,128)} %param.8) | copy-start | bytes 24580
  45.6 1.6 copy-start.1
  47.2 11.9 %copy-start.5 = (bf16[2048,128]{1,0:T(8,128)(2,1)S(1)}, bf16[2048,128]{1,0:T(8,128)(2,1)}, u32[]{:S(2)}) copy-start(bf16[2048,128]{1,0:T(8,128)(2,1)} %get-tuple-element.46.basis_t_ref) | copy-start | bytes 1572868
  48.5 10.5 %collective-permute-start = (f32[8,512]{1,0:T(8,128)S(1)}, f32[8,512]{1,0:T(8,128)S(1)}, u32[]{:S(2)}, u32[]{:S(2)}) collective-permute-start(f32[8,512]{1,0:T(8,128)S(1)} %get-tuple-element.42), channel_id=1, source_target_pairs={{0,128},{128,256},{256,384},{384,512},{512,640},{640,768},{768,896... | collective-permute-start | bytes 49160 | tf_op jit(solution)/shard_map/ppermute | solution.py:401
  51.7 7.3 %collective-permute-start.1 = (f32[8,512]{1,0:T(8,128)S(1)}, f32[8,512]{1,0:T(8,128)S(1)}, u32[]{:S(2)}, u32[]{:S(2)}) collective-permute-start(f32[8,512]{1,0:T(8,128)S(1)} %get-tuple-element.43), channel_id=1, source_target_pairs={{128,0},{256,128},{384,256},{512,384},{640,512},{768,640},{896,768... | collective-permute-start | bytes 49160 | tf_op jit(solution)/shard_map/ppermute | solution.py:402
  53.0 6.0 %collective-permute-start.2 = (f32[8,512]{1,0:T(8,128)S(1)}, f32[8,512]{1,0:T(8,128)S(1)}, u32[]{:S(2)}, u32[]{:S(2)}) collective-permute-start(f32[8,512]{1,0:T(8,128)S(1)} %get-tuple-element.44), channel_id=1, source_target_pairs={{1,2},{2,1},{3,4},{4,3},{5,6},{6,5},{7,8},{8,7},{9,10},{10,9},{11,... | collective-permute-start | bytes 49160 | tf_op jit(solution)/shard_map/ppermute | solution.py:403
  55.7 3.4 %collective-permute-start.3 = (f32[8,512]{1,0:T(8,128)S(1)}, f32[8,512]{1,0:T(8,128)S(1)}, u32[]{:S(2)}, u32[]{:S(2)}) collective-permute-start(f32[8,512]{1,0:T(8,128)S(1)} %get-tuple-element.45), channel_id=1, source_target_pairs={{0,1},{1,0},{2,3},{3,2},{4,5},{5,4},{6,7},{7,6},{8,9},{9,8},{10,11... | collective-permute-start | bytes 49160 | tf_op jit(solution)/shard_map/ppermute | solution.py:404
  57.7 29.6 %copy-start.2 = (bf16[8192,128]{1,0:T(8,128)(2,1)S(1)}, bf16[8192,128]{1,0:T(8,128)(2,1)}, u32[]{:S(2)}) copy-start(bf16[8192,128]{1,0:T(8,128)(2,1)} %copy-done) | copy-start | bytes 6291460
  88.6 11.5 %collective-permute-start.4 = (f32[8,512]{1,0:T(8,128)S(1)}, f32[8,512]{1,0:T(8,128)S(1)}, u32[]{:S(2)}, u32[]{:S(2)}) collective-permute-start(f32[8,512]{1,0:T(8,128)S(1)} %get-tuple-element.50), channel_id=1, source_target_pairs={{0,128},{128,256},{256,384},{384,512},{512,640},{640,768},{768,896... | collective-permute-start | bytes 49160 | tf_op jit(solution)/shard_map/ppermute | solution.py:401
  92.9 7.2 %collective-permute-start.5 = (f32[8,512]{1,0:T(8,128)S(1)}, f32[8,512]{1,0:T(8,128)S(1)}, u32[]{:S(2)}, u32[]{:S(2)}) collective-permute-start(f32[8,512]{1,0:T(8,128)S(1)} %get-tuple-element.51), channel_id=1, source_target_pairs={{128,0},{256,128},{384,256},{512,384},{640,512},{768,640},{896,768... | collective-permute-start | bytes 49160 | tf_op jit(solution)/shard_map/ppermute | solution.py:402
  94.2 5.9 %collective-permute-start.6 = (f32[8,512]{1,0:T(8,128)S(1)}, f32[8,512]{1,0:T(8,128)S(1)}, u32[]{:S(2)}, u32[]{:S(2)}) collective-permute-start(f32[8,512]{1,0:T(8,128)S(1)} %get-tuple-element.52), channel_id=1, source_target_pairs={{1,2},{2,1},{3,4},{4,3},{5,6},{6,5},{7,8},{8,7},{9,10},{10,9},{11,... | collective-permute-start | bytes 49160 | tf_op jit(solution)/shard_map/ppermute | solution.py:403
  96.9 3.3 %collective-permute-start.7 = (f32[8,512]{1,0:T(8,128)S(1)}, f32[8,512]{1,0:T(8,128)S(1)}, u32[]{:S(2)}, u32[]{:S(2)}) collective-permute-start(f32[8,512]{1,0:T(8,128)S(1)} %get-tuple-element.53), channel_id=1, source_target_pairs={{0,1},{1,0},{2,3},{3,2},{4,5},{5,4},{6,7},{7,6},{8,9},{9,8},{10,11... | collective-permute-start | bytes 49160 | tf_op jit(solution)/shard_map/ppermute | solution.py:404
  129.7 11.5 %collective-permute-start.8 = (f32[8,512]{1,0:T(8,128)S(1)}, f32[8,512]{1,0:T(8,128)S(1)}, u32[]{:S(2)}, u32[]{:S(2)}) collective-permute-start(f32[8,512]{1,0:T(8,128)S(1)} %get-tuple-element.57), channel_id=1, source_target_pairs={{0,128},{128,256},{256,384},{384,512},{512,640},{640,768},{768,896... | collective-permute-start | bytes 49160 | tf_op jit(solution)/shard_map/ppermute | solution.py:401
  133.9 7.2 %collective-permute-start.9 = (f32[8,512]{1,0:T(8,128)S(1)}, f32[8,512]{1,0:T(8,128)S(1)}, u32[]{:S(2)}, u32[]{:S(2)}) collective-permute-start(f32[8,512]{1,0:T(8,128)S(1)} %get-tuple-element.58), channel_id=1, source_target_pairs={{128,0},{256,128},{384,256},{512,384},{640,512},{768,640},{896,768... | collective-permute-start | bytes 49160 | tf_op jit(solution)/shard_map/ppermute | solution.py:402
  135.2 5.9 %collective-permute-start.10 = (f32[8,512]{1,0:T(8,128)S(1)}, f32[8,512]{1,0:T(8,128)S(1)}, u32[]{:S(2)}, u32[]{:S(2)}) collective-permute-start(f32[8,512]{1,0:T(8,128)S(1)} %get-tuple-element.59), channel_id=1, source_target_pairs={{1,2},{2,1},{3,4},{4,3},{5,6},{6,5},{7,8},{8,7},{9,10},{10,9},{11,... | collective-permute-start | bytes 49160 | tf_op jit(solution)/shard_map/ppermute | solution.py:403
  137.9 3.3 %collective-permute-start.11 = (f32[8,512]{1,0:T(8,128)S(1)}, f32[8,512]{1,0:T(8,128)S(1)}, u32[]{:S(2)}, u32[]{:S(2)}) collective-permute-start(f32[8,512]{1,0:T(8,128)S(1)} %get-tuple-element.60), channel_id=1, source_target_pairs={{0,1},{1,0},{2,3},{3,2},{4,5},{5,4},{6,7},{7,6},{8,9},{9,8},{10,11... | collective-permute-start | bytes 49160 | tf_op jit(solution)/shard_map/ppermute | solution.py:404

commit v4 on v3

--- a/solution.py
+++ b/solution.py
@@ -73,35 +73,41 @@
     return jnp.concatenate(parts, axis=0).T.astype(BF16)
 
 
-def start_kernel(
-    core_ref, rhs_hbm, basis_hbm, diag_hbm, basis_t_ref, basis_h_ref, inv_ref, piece_ref,
-    rhs_ref, basis_ref, diag_ref, sems,
-):
+def start_kernel(core_ref, rhs_hbm, basis_hbm, piece_ref, rhs_ref, basis_ref, sems):
     copies = [
         pltpu.make_async_copy(source, target, sems.at[i])
-        for i, (source, target) in enumerate(
-            ((basis_hbm, basis_ref), (rhs_hbm, rhs_ref), (diag_hbm, diag_ref))
-        )
+        for i, (source, target) in enumerate(((basis_hbm, basis_ref), (rhs_hbm, rhs_ref)))
     ]
     for copy in copies:
         copy.start()
+    for copy in copies:
+        copy.wait()
     gen, rows = basis_ref.shape
-    copies[0].wait()
+    basis_t = jnp.concatenate(
+        [
+            transposed_halves(basis_ref[:, t * LANES : (t + 1) * LANES])
+            for t in range(rows // LANES)
+        ],
+        axis=0,
+    )
+    piece = coarse_piece(rhs_ref[...], basis_t, core_ref[0], gen)
+    for t in range(piece_ref.shape[0]):
+        piece_ref[t] = piece
+
+
+def prepare_kernel(basis_ref, diag_ref, blocks_ref, basis_t_ref, basis_h_ref, inv_ref, weights_ref):
+    rows = basis_ref.shape[1]
     for t in range(rows // LANES):
         cols = slice(t * LANES, (t + 1) * LANES)
         basis_t_ref[cols, :] = transposed_halves(basis_ref[:, cols])
-    copies[1].wait()
-    piece = coarse_piece(rhs_ref[...], basis_t_ref[...], core_ref[0], gen)
-    for t in range(piece_ref.shape[0]):
-        piece_ref[t] = piece
     high, low = halves(basis_ref[...])
     basis_h_ref[:, :rows] = high.astype(BF16)
     basis_h_ref[:, rows:] = low.astype(BF16)
-    copies[2].wait()
     inv_ref[...] = 1.0 / diag_ref[...]
-
-
-def coarse_kernel(inverse_ref, out_ref):
+    block_kernel(blocks_ref, weights_ref)
+
+
+def coarse_kernel(after_ref, inverse_ref, out_ref):
     gen, total = inverse_ref.shape
     zero = jnp.zeros((HALF - gen, LANES), BF16)
     for t in range(total // (2 * gen)):
@@ -132,14 +138,9 @@
     lax.fori_loop(0, nblocks // 2, step, 0)
 
 
-def prepare_kernel(inverse_ref, blocks_ref, coarse_ref, weights_ref):
-    coarse_kernel(inverse_ref, coarse_ref)
-    block_kernel(blocks_ref, weights_ref)
-
-
 def field_kernel(
     core_ref, margin_ref, pieces_ref, k_ref, inv_ref, coarse_ref, basis_h_ref,
-    p_ref, up_ref, down_ref, across_ref, partner_ref, packed_ref,
+    p_ref, rims_ref, across_ref, packed_ref,
 ):
     count, rows = k_ref.shape
     gen = basis_h_ref.shape[0]
@@ -162,7 +163,9 @@
         k_ref[...] * inv_ref[...] + (back[:count, :rows] + back[count:, :rows]) + back[:count, rows:]
     )
     core = core_ref[0]
-    for rim_ref, d in ((up_ref, 1), (down_ref, 0), (across_ref, 2 + core), (partner_ref, 3 - core)):
+    for rim_ref, d in (
+        (rims_ref.at[0], 1), (rims_ref.at[1], 0), (rims_ref.at[2], 3 - core), (across_ref, 2 + core)
+    ):
         for j in range(margin_ref.shape[1]):
             tile = margin_ref[d, j]
             rim_ref[:, j * LANES : (j + 1) * LANES] = p_ref[
@@ -199,10 +202,15 @@
         out_ref[:, cols] = diag_ref[:, cols] * p_ref[:, cols] + local
 
 
-def couple(core_ref, margin_ref, base_ref, low_ref, high_ref, across_ref, partner_ref, k_ref):
+def couple(core_ref, margin_ref, base_ref, vertical_ref, across_ref, pair_ref, k_ref):
     core = core_ref[0]
     k_ref[...] = base_ref[...]
-    for d, source in ((0, low_ref), (1, high_ref), (2 + core, across_ref), (3 - core, partner_ref)):
+    for d, source in (
+        (0, vertical_ref.at[0, core]),
+        (1, vertical_ref.at[1, core]),
+        (2 + core, across_ref),
+        (3 - core, pair_ref.at[1 - core, 2]),
+    ):
         for j in range(margin_ref.shape[1]):
             at = pl.ds(pl.multiple_of(margin_ref[d, j] * LANES, LANES), LANES)
             k_ref[:, at] = k_ref[:, at] - source[:, j * LANES : (j + 1) * LANES]
@@ -210,20 +218,20 @@
 
 
 def next_kernel(
-    gen, core_ref, margin_ref, base_ref, low_ref, high_ref, across_ref, partner_ref, basis_t_ref,
+    gen, core_ref, margin_ref, base_ref, vertical_ref, across_ref, pair_ref, basis_t_ref,
     k_ref, piece_ref,
 ):
-    couple(core_ref, margin_ref, base_ref, low_ref, high_ref, across_ref, partner_ref, k_ref)
+    couple(core_ref, margin_ref, base_ref, vertical_ref, across_ref, pair_ref, k_ref)
     piece = coarse_piece(k_ref[...], basis_t_ref[...], core_ref[0], gen)
     for t in range(piece_ref.shape[0]):
         piece_ref[t] = piece
 
 
 def gram_kernel(
-    core_ref, margin_ref, base_ref, low_ref, high_ref, across_ref, partner_ref, k0_ref, k1_ref, k2_ref,
+    core_ref, margin_ref, base_ref, vertical_ref, across_ref, pair_ref, k0_ref, k1_ref, k2_ref,
     sums_ref, k3_ref,
 ):
-    couple(core_ref, margin_ref, base_ref, low_ref, high_ref, across_ref, partner_ref, k3_ref)
+    couple(core_ref, margin_ref, base_ref, vertical_ref, across_ref, pair_ref, k3_ref)
     fields = [k0_ref[...], k1_ref[...], k2_ref[...], k3_ref[...]]
     count = fields[0].shape[0]
     lane = lane_of((count, LANES))
@@ -346,40 +354,42 @@
     subs = lax.axis_size(SUB)
     rim = margin.shape[1] * LANES
     core = lax.axis_index("core").astype(jnp.int32).reshape(1)
-    up = [(i, i + 1) for i in range(groups - 1)]
-    down = [(j, i) for i, j in up]
+    vertical = [(2 * g, 2 * g + 2) for g in range(groups - 1)]
+    vertical += [(2 * g + 3, 2 * g + 1) for g in range(groups - 1)]
     across = [(i, ((i + 1) ^ 1) - 1) for i in range(1, subs - 1)]
     wide = subs * HALF
 
     chips = zs * xs
     anywhere = pl.BlockSpec(memory_space=pl.ANY)
 
-    basis_t, basis_h, inv_row, piece = call(
+    piece = call(
         start_kernel,
-        [
-            shape(rows, LANES, dtype=BF16),
-            shape(gen, 2 * rows, dtype=BF16),
-            shape(1, rows),
-            shape(chips, count // 2, LANES),
-        ],
-        [smem(), anywhere, anywhere, anywhere],
+        shape(chips, count // 2, LANES),
+        [smem(), anywhere, anywhere],
         3_000_000,
         1_500_000,
         [
             pltpu.VMEM((count, rows), F32),
             pltpu.VMEM((gen, rows), F32),
-            pltpu.VMEM((1, rows), F32),
-            pltpu.SemaphoreType.DMA((3,)),
+            pltpu.SemaphoreType.DMA((2,)),
         ],
         60,
-    )(core, source, basis, diag_row)
-    coarse, weights = call(
+    )(core, source, basis)
+    basis_t, basis_h, inv_row, weights = call(
         prepare_kernel,
-        [shape(wide, LANES, dtype=BF16), shape(nblocks, 4 * HALF, LANES, dtype=BF16)],
-        [vmem(), vmem()],
+        [
+            shape(rows, LANES, dtype=BF16),
+            shape(gen, 2 * rows, dtype=BF16),
+            shape(1, rows),
+            shape(nblocks, 4 * HALF, LANES, dtype=BF16),
+        ],
+        [vmem()] * 3,
         2_000_000,
-        8_000_000,
-    )(inverse, blocks[0, 0])
+        6_000_000,
+    )(basis, diag_row, blocks[0, 0])
+    coarse = call(
+        coarse_kernel, shape(wide, LANES, dtype=BF16), [anywhere, vmem()], 1_000_000, 3_200_000
+    )(inv_row, inverse)
 
     krylov = [source]
     conditioned = []
@@ -387,21 +397,21 @@
     for step in range(ITERS):
         pieces = spread(piece, ("z", "x"))
         if step == 0:
-            pieces, coarse, weights = lax.optimization_barrier((pieces, coarse, weights))
+            pieces, weights = lax.optimization_barrier((pieces, weights))
         pieces = lax.all_gather(pieces, "core")
-        p, send_up, send_down, send_across, send_partner = call(
+        p, rims, send_across = call(
             field_kernel,
-            [shape(count, rows)] + [shape(count, rim)] * 4,
+            [shape(count, rows), shape(3, count, rim), shape(count, rim)],
             [smem(), smem()] + [vmem()] * 5,
             8_000_000,
             3_500_000,
             [pltpu.VMEM((2 * count, wide), BF16)],
         )(core, margin, pieces, krylov[-1], inv_row, coarse, basis_h)
         conditioned.append(p)
-        from_low = lax.ppermute(send_up, "grp", up)
-        from_high = lax.ppermute(send_down, "grp", down)
         other = lax.ppermute(send_across, SUB, across)
-        partner = lax.ppermute(send_partner, "core", [(0, 1), (1, 0)])
+        pair = lax.all_gather(rims, "core")
+        carried = lax.dynamic_index_in_dim(pair, core[0], axis=1, keepdims=False)
+        carried = lax.ppermute(carried, ("grp", "core"), vertical)
         base = call(
             local_kernel,
             shape(count, rows),
@@ -410,12 +420,12 @@
             2_500_000,
             [pltpu.VMEM((nblocks, 2 * count, LANES), BF16)] * 2,
         )(pattern, p, diag_row, weights)
-        shared = (core, margin, base, from_low, from_high, other, partner)
+        shared = (core, margin, base, lax.all_gather(carried, "core"), other, pair)
         if step < ITERS - 1:
             field, piece = call(
                 functools.partial(next_kernel, gen),
                 [shape(count, rows), shape(chips, count // 2, LANES)],
-                [smem(), smem()] + [vmem()] * 6,
+                [smem(), smem()] + [vmem()] * 5,
                 4_000_000,
                 1_000_000,
             )(*shared, basis_t)
@@ -424,7 +434,7 @@
             sums = call(
                 gram_kernel,
                 shape(chips, 1, LANES),
-                [smem(), smem()] + [vmem()] * 8,
+                [smem(), smem()] + [vmem()] * 7,
                 400_000,
                 500_000,
                 [pltpu.VMEM((count, rows), F32)],

time: 185 us -> 177 us (0.957)
  starting transfers between devices: 52.1 us -> 40.5 us
  blocking collectives: 101 us -> 105 us
    ppermute x9 -> x3, starting transfers between devices: 21.4 us -> 3.84 us  [per_device(): carried = lax.ppermute(carried, ('grp', 'core'), vertical)]
    all_gather x0 -> x6, blocking collectives: none -> 11.2 us  [the longest x3 5.67 us: per_device(): pair = lax.all_gather(rims, 'core')]
    all_to_all x4, blocking collectives: 85.4 us -> 79.4 us  [spread(): return lax.all_to_all(value, axis, 0, 0)]
    ppermute x3, starting transfers between devices: 7.93 us -> 13.8 us  [per_device(): other = lax.ppermute(send_across, SUB, across)]
    unnamed x24 -> x22, local copies, waits for them, and re-layouts: 6.11 us -> 6.51 us
    pallas_call x6 -> x7, Pallas kernels: 10.7 us -> 10.6 us  [the longest x3 3.88 us: per_device(): call(field_kernel, [shape(count, rows), shape(3, count, rim), shape(count...]
  transfers between devices with their start and end apart: 13 -> 7, of which waited for: 1 -> 1; matrix products, arithmetic and copies ran while one was open for 0% -> 0% of each run, Pallas kernels for 4% -> 4%
where the time goes in v4:
time: 177 us; the launch traced here: 176 us
  blocking collectives  105 us (59%)
  starting transfers between devices  40.5 us (23%)
  Pallas kernels  17.2 us (10%)
  local copies, waits for them, and re-layouts  6.62 us (4%)
  waiting for transfers between devices  6.15 us (3%)
    all_to_all x4, blocking collectives, spread(): return lax.all_to_all(value, axis, 0, 0)  79.4 us
    all_to_all x1, starting transfers between devices, spread(): return lax.all_to_all(value, axis, 0, 0)  22.8 us
    all_gather x3, blocking collectives, per_device(): pieces = lax.all_gather(pieces, 'core')  14.5 us
    ppermute x3, starting transfers between devices, per_device(): other = lax.ppermute(send_across, SUB, across)  13.8 us
    unnamed x22, local copies, waits for them, and re-layouts  6.51 us
    all_to_all x1, waiting for transfers between devices, spread(): return lax.all_to_all(value, axis, 0, 0)  6.13 us
    all_gather x3, blocking collectives, per_device(): pair = lax.all_gather(rims, 'core')  5.67 us
    all_gather x3, blocking collectives, per_device(): shared = (core, margin, base, lax.all_gather(carried, 'core'), other, pair)  5.56 us
  transfers between devices with their start and end apart: 7, of which 1 were waited for; matrix products, arithmetic and copies ran while one was open for 0% of the time, Pallas kernels for 4%

profile of v4, /device:TPU:1, one launch (start us, length us, event | category | flops | bytes accessed | tf_op | source)
XLA Modules:
  0.0 175.9 jit_solution(3767103485742462687)
XLA Ops:
  0.0 2.1 %shard_map.73 = f32[64,4,128]{2,1,0:T(4,128)} custom-call(s32[1]{0:T(128)} %bitcast.core_ref, f32[8,2048]{1,0:T(8,128)} %bitcast.31, f32[48,2048]{1,0:T(8,128)} %bitcast.25), custom_call_target="tpu_custom_call" | custom-call | flops 3000000 | bytes 1500000 | tf_op jit(solution)/shard_map/pallas_call | solution.py:365
  2.1 22.8 %all-to-all-start = ((f32[64,4,128]{2,1,0:T(4,128)}), f32[64,4,128]{2,1,0:T(4,128)S(1)}, u32[]{:S(2)}, u32[]{:S(2)}) async-start(f32[64,4,128]{2,1,0:T(4,128)} %shard_map.73), calls=%async_computation | async-start | bytes 262144 | tf_op jit(solution)/shard_map/all_to_all | solution.py:264
  24.9 1.9 %copy-done.3 = f32[1,1,32,3,64,64]{5,4,3,2,1,0:T(8,128)S(1)} copy-done((f32[1,1,32,3,64,64]{5,4,3,2,1,0:T(8,128)S(1)}, f32[1,1,32,3,64,64]{5,4,3,2,1,0:T(8,128)}, u32[]{:S(2)}) %copy-start.3) | copy-done | bytes 1572888
  28.5 2.2 %shard_map.74 = (bf16[2048,128]{1,0:T(8,128)(2,1)S(1)}, bf16[48,4096]{1,0:T(8,128)(2,1)S(1)}, f32[1,2048]{1,0:T(1,128)S(1)}, bf16[32,256,128]{2,1,0:T(8,128)(2,1)S(1)}) custom-call(f32[48,2048]{1,0:T(8,128)S(1)} %bitcast.26, f32[1,2048]{1,0:T(1,128)S(1)} %bitcast.46, f32[32,3,64,64]{3,2,1,0:T(8,128)S(1)} %bitcast.24), custom_call_target="tpu_custom_call" | custom-call | flops 2000000 | bytes 6000000 | tf_op jit(solution)/shard_map/pallas_call | solution.py:378
  30.7 1.3 copy-done
  32.1 1.6 shard_map.75.coarse_ref
  33.7 6.1 %all-to-all-done = f32[64,4,128]{2,1,0:T(4,128)S(1)} async-done(((f32[64,4,128]{2,1,0:T(4,128)}), f32[64,4,128]{2,1,0:T(4,128)S(1)}, u32[]{:S(2)}, u32[]{:S(2)}) %all-to-all-start) | async-done | bytes 131104 | tf_op jit(solution)/shard_map/all_to_all | solution.py:264
  39.8 5.4 %all-gather = f32[128,4,128]{2,1,0:T(4,128)S(1)} all-gather(f32[64,4,128]{2,1,0:T(4,128)S(1)} %all-to-all-done), channel_id=2, replica_groups=mesh['grp'=8,'z'=16,'x'=4,'core'=2] {'core'}, dimensions={0}, use_global_device_ids=true | all-gather | bytes 393216 | tf_op jit(solution)/shard_map/all_gather | solution.py:401
  45.2 1.3 shard_map.76
  46.5 1.9 %all-gather.1 = f32[6,8,512]{2,1,0:T(8,128)S(1)} all-gather(f32[3,8,512]{2,1,0:T(8,128)S(1)} %get-tuple-element.30), channel_id=3, replica_groups=mesh['grp'=8,'z'=16,'x'=4,'core'=2] {'core'}, dimensions={0}, use_global_device_ids=true | all-gather | bytes 147456 | tf_op jit(solution)/shard_map/all_gather | solution.py:412
  48.4 1.3 collective-permute-start
  49.7 4.5 %collective-permute-start.1 = (f32[8,512]{1,0:T(8,128)S(1)}, f32[8,512]{1,0:T(8,128)S(1)}, u32[]{:S(2)}, u32[]{:S(2)}) collective-permute-start(f32[8,512]{1,0:T(8,128)S(1)} %get-tuple-element.31), channel_id=1, source_target_pairs={{1,2},{2,1},{3,4},{4,3},{5,6},{6,5},{7,8},{8,7},{9,10},{10,9},{11,... | collective-permute-start | bytes 49160 | tf_op jit(solution)/shard_map/ppermute | solution.py:411
  54.3 1.6 copy-done.1
  55.9 1.3 shard_map.77.base_ref
  57.2 1.9 %all-gather.2 = f32[4,8,512]{2,1,0:T(8,128)S(1)} all-gather(f32[2,8,512]{2,1,0:T(8,128)S(1)} %collective-permute-done), channel_id=4, replica_groups=mesh['grp'=8,'z'=16,'x'=4,'core'=2] {'core'}, dimensions={0}, use_global_device_ids=true | all-gather | bytes 98304 | tf_op jit(solution)/shard_map/all_gather | solution.py:423
  60.0 22.7 %all_to_all.25 = f32[64,4,128]{2,1,0:T(4,128)S(1)} all-to-all(f32[64,4,128]{2,1,0:T(4,128)S(1)} %get-tuple-element.33), channel_id=1, replica_groups=mesh['grp'=8,'z'=16,'x'=4,'core'=2] {'z','x'}, dimensions={0} | all-to-all | bytes 262144 | tf_op jit(solution)/shard_map/all_to_all | solution.py:264
  82.6 4.6 %all-gather.3 = f32[128,4,128]{2,1,0:T(4,128)S(1)} all-gather(f32[64,4,128]{2,1,0:T(4,128)S(1)} %all_to_all.25), channel_id=5, replica_groups=mesh['grp'=8,'z'=16,'x'=4,'core'=2] {'core'}, dimensions={0}, use_global_device_ids=true | all-gather | bytes 393216 | tf_op jit(solution)/shard_map/all_gather | solution.py:401
  87.2 1.3 shard_map.79
  88.5 1.9 %all-gather.4 = f32[6,8,512]{2,1,0:T(8,128)S(1)} all-gather(f32[3,8,512]{2,1,0:T(8,128)S(1)} %get-tuple-element.36), channel_id=6, replica_groups=mesh['grp'=8,'z'=16,'x'=4,'core'=2] {'core'}, dimensions={0}, use_global_device_ids=true | all-gather | bytes 147456 | tf_op jit(solution)/shard_map/all_gather | solution.py:412
  90.4 1.3 collective-permute-start.2
  91.7 4.7 %collective-permute-start.3 = (f32[8,512]{1,0:T(8,128)S(1)}, f32[8,512]{1,0:T(8,128)S(1)}, u32[]{:S(2)}, u32[]{:S(2)}) collective-permute-start(f32[8,512]{1,0:T(8,128)S(1)} %get-tuple-element.37), channel_id=1, source_target_pairs={{1,2},{2,1},{3,4},{4,3},{5,6},{6,5},{7,8},{8,7},{9,10},{10,9},{11,... | collective-permute-start | bytes 49160 | tf_op jit(solution)/shard_map/ppermute | solution.py:411
  96.4 1.3 shard_map.80.base_ref
  97.7 1.9 %all-gather.5 = f32[4,8,512]{2,1,0:T(8,128)S(1)} all-gather(f32[2,8,512]{2,1,0:T(8,128)S(1)} %collective-permute-done.2), channel_id=7, replica_groups=mesh['grp'=8,'z'=16,'x'=4,'core'=2] {'core'}, dimensions={0}, use_global_device_ids=true | all-gather | bytes 98304 | tf_op jit(solution)/shard_map/all_gather | solution.py:423
  100.5 22.6 %all_to_all.26 = f32[64,4,128]{2,1,0:T(4,128)S(1)} all-to-all(f32[64,4,128]{2,1,0:T(4,128)S(1)} %get-tuple-element.38), channel_id=1, replica_groups=mesh['grp'=8,'z'=16,'x'=4,'core'=2] {'z','x'}, dimensions={0} | all-to-all | bytes 262144 | tf_op jit(solution)/shard_map/all_to_all | solution.py:264
  123.1 4.6 %all-gather.6 = f32[128,4,128]{2,1,0:T(4,128)S(1)} all-gather(f32[64,4,128]{2,1,0:T(4,128)S(1)} %all_to_all.26), channel_id=8, replica_groups=mesh['grp'=8,'z'=16,'x'=4,'core'=2] {'core'}, dimensions={0}, use_global_device_ids=true | all-gather | bytes 393216 | tf_op jit(solution)/shard_map/all_gather | solution.py:401
  127.7 1.3 shard_map.82
  129.0 1.9 %all-gather.7 = f32[6,8,512]{2,1,0:T(8,128)S(1)} all-gather(f32[3,8,512]{2,1,0:T(8,128)S(1)} %get-tuple-element.41), channel_id=9, replica_groups=mesh['grp'=8,'z'=16,'x'=4,'core'=2] {'core'}, dimensions={0}, use_global_device_ids=true | all-gather | bytes 147456 | tf_op jit(solution)/shard_map/all_gather | solution.py:412
  132.2 4.7 %collective-permute-start.5 = (f32[8,512]{1,0:T(8,128)S(1)}, f32[8,512]{1,0:T(8,128)S(1)}, u32[]{:S(2)}, u32[]{:S(2)}) collective-permute-start(f32[8,512]{1,0:T(8,128)S(1)} %get-tuple-element.42), channel_id=1, source_target_pairs={{1,2},{2,1},{3,4},{4,3},{5,6},{6,5},{7,8},{8,7},{9,10},{10,9},{11,... | collective-permute-start | bytes 49160 | tf_op jit(solution)/shard_map/ppermute | solution.py:411
  136.9 1.3 shard_map.83.base_ref
  138.2 1.9 %all-gather.8 = f32[4,8,512]{2,1,0:T(8,128)S(1)} all-gather(f32[2,8,512]{2,1,0:T(8,128)S(1)} %collective-permute-done.4), channel_id=10, replica_groups=mesh['grp'=8,'z'=16,'x'=4,'core'=2] {'core'}, dimensions={0}, use_global_device_ids=true | all-gather | bytes 98304 | tf_op jit(solution)/shard_map/all_gather | solution.py:423
  140.9 20.5 %all_to_all.27 = f32[64,1,128]{2,1,0:T(1,128)S(1)} all-to-all(f32[64,1,128]{2,1,0:T(1,128)S(1)} %shard_map.84), channel_id=1, replica_groups=mesh['grp'=8,'z'=16,'x'=4,'core'=2] {'z','x'}, dimensions={0} | all-to-all | bytes 65536 | tf_op jit(solution)/shard_map/all_to_all | solution.py:264
  161.5 13.6 %all_to_all.28.sums_ref = f32[16,1,128]{2,1,0:T(1,128)S(1)} all-to-all(f32[16,1,128]{2,1,0:T(1,128)S(1)} %broadcast_in_dim.4), channel_id=1, replica_groups=mesh['grp'=8,'z'=16,'x'=4,'core'=2] {'grp','core'}, dimensions={0} | all-to-all | bytes 16384 | tf_op jit(solution)/shard_map/all_to_all | solution.py:264
  (36 shorter events, 6.6 us)
Async XLA Ops:
  2.1 37.7 %all-to-all-start = ((f32[64,4,128]{2,1,0:T(4,128)}), f32[64,4,128]{2,1,0:T(4,128)S(1)}, u32[]{:S(2)}, u32[]{:S(2)}) async-start(f32[64,4,128]{2,1,0:T(4,128)} %shard_map.73), calls=%async_computation | async-start | bytes 262144 | tf_op jit(solution)/shard_map/all_to_all | solution.py:264
  24.9 1.9 %copy-start.3 = (f32[1,1,32,3,64,64]{5,4,3,2,1,0:T(8,128)S(1)}, f32[1,1,32,3,64,64]{5,4,3,2,1,0:T(8,128)}, u32[]{:S(2)}) copy-start(f32[1,1,32,3,64,64]{5,4,3,2,1,0:T(8,128)} %param.9) | copy-start | bytes 4718596
  26.8 1.0 copy-start.4
  27.8 0.7 copy-start.7
  28.5 3.6 %copy-start.5 = (f32[1,48,6144]{2,1,0:T(8,128)S(1)}, f32[1,48,6144]{2,1,0:T(8,128)}, u32[]{:S(2)}) copy-start(f32[1,48,6144]{2,1,0:T(8,128)} %param.13) | copy-start | bytes 3538948
  30.7 1.3 copy-start
  32.1 13.1 %copy-start.6 = (f32[1,1,8,2048]{3,2,1,0:T(8,128)S(1)}, f32[1,1,8,2048]{3,2,1,0:T(8,128)}, u32[]{:S(2)}) copy-start(f32[1,1,8,2048]{3,2,1,0:T(8,128)} %param.7) | copy-start | bytes 196612
  32.1 13.1 %copy-start.9 = (s32[1,1,4,4]{3,2,1,0:T(4,128)S(1)}, s32[1,1,4,4]{3,2,1,0:T(4,128)}, u32[]{:S(2)}) copy-start(s32[1,1,4,4]{3,2,1,0:T(4,128)} %param.11) | copy-start | bytes 196
  33.6 16.0 %copy-start.10 = (s32[1,1,32,3]{2,1,3,0:T(1,128)S(1)}, s32[1,1,32,3]{2,1,3,0:T(1,128)}, u32[]{:S(2)}) copy-start(s32[1,1,32,3]{2,1,3,0:T(1,128)} %param.10) | copy-start | bytes 1156
  33.7 20.6 %copy-start.8 = (f32[1,1,2048]{2,1,0:T(1,128)S(1)}, f32[1,1,2048]{2,1,0:T(1,128)}, u32[]{:S(2)}) copy-start(f32[1,1,2048]{2,1,0:T(1,128)} %param.8) | copy-start | bytes 24580
  48.4 8.9 %collective-permute-start = (f32[2,8,512]{2,1,0:T(8,128)S(1)}, f32[2,8,512]{2,1,0:T(8,128)S(1)}, u32[]{:S(2)}, u32[]{:S(2)}) collective-permute-start(f32[2,8,512]{2,1,0:T(8,128)S(1)} %dynamic-slice_bitcast_fusion.2), channel_id=1, source_target_pairs={{0,128},{128,256},{256,384},{384,512},{512,640},{640,768},{768,896... | collective-permute-start | bytes 98312 | tf_op jit(solution)/shard_map/ppermute | solution.py:414
  49.7 9.3 %collective-permute-start.1 = (f32[8,512]{1,0:T(8,128)S(1)}, f32[8,512]{1,0:T(8,128)S(1)}, u32[]{:S(2)}, u32[]{:S(2)}) collective-permute-start(f32[8,512]{1,0:T(8,128)S(1)} %get-tuple-element.31), channel_id=1, source_target_pairs={{1,2},{2,1},{3,4},{4,3},{5,6},{6,5},{7,8},{8,7},{9,10},{10,9},{11,... | collective-permute-start | bytes 49160 | tf_op jit(solution)/shard_map/ppermute | solution.py:411
  54.3 1.6 copy-start.1
  59.1 37.3 %copy-start.2 = (bf16[32,256,128]{2,1,0:T(8,128)(2,1)S(1)}, bf16[32,256,128]{2,1,0:T(8,128)(2,1)}, u32[]{:S(2)}) copy-start(bf16[32,256,128]{2,1,0:T(8,128)(2,1)} %copy-done) | copy-start | bytes 6291460
  90.4 7.3 %collective-permute-start.2 = (f32[2,8,512]{2,1,0:T(8,128)S(1)}, f32[2,8,512]{2,1,0:T(8,128)S(1)}, u32[]{:S(2)}, u32[]{:S(2)}) collective-permute-start(f32[2,8,512]{2,1,0:T(8,128)S(1)} %dynamic-slice_bitcast_fusion.1), channel_id=1, source_target_pairs={{0,128},{128,256},{256,384},{384,512},{512,640},{640,768},{768,896... | collective-permute-start | bytes 98312 | tf_op jit(solution)/shard_map/ppermute | solution.py:414
  91.7 7.9 %collective-permute-start.3 = (f32[8,512]{1,0:T(8,128)S(1)}, f32[8,512]{1,0:T(8,128)S(1)}, u32[]{:S(2)}, u32[]{:S(2)}) collective-permute-start(f32[8,512]{1,0:T(8,128)S(1)} %get-tuple-element.37), channel_id=1, source_target_pairs={{1,2},{2,1},{3,4},{4,3},{5,6},{6,5},{7,8},{8,7},{9,10},{10,9},{11,... | collective-permute-start | bytes 49160 | tf_op jit(solution)/shard_map/ppermute | solution.py:411
  130.9 7.3 %collective-permute-start.4 = (f32[2,8,512]{2,1,0:T(8,128)S(1)}, f32[2,8,512]{2,1,0:T(8,128)S(1)}, u32[]{:S(2)}, u32[]{:S(2)}) collective-permute-start(f32[2,8,512]{2,1,0:T(8,128)S(1)} %dynamic-slice_bitcast_fusion), channel_id=1, source_target_pairs={{0,128},{128,256},{256,384},{384,512},{512,640},{640,768},{768,896... | collective-permute-start | bytes 98312 | tf_op jit(solution)/shard_map/ppermute | solution.py:414
  132.2 7.9 %collective-permute-start.5 = (f32[8,512]{1,0:T(8,128)S(1)}, f32[8,512]{1,0:T(8,128)S(1)}, u32[]{:S(2)}, u32[]{:S(2)}) collective-permute-start(f32[8,512]{1,0:T(8,128)S(1)} %get-tuple-element.42), channel_id=1, source_target_pairs={{1,2},{2,1},{3,4},{4,3},{5,6},{6,5},{7,8},{8,7},{9,10},{10,9},{11,... | collective-permute-start | bytes 49160 | tf_op jit(solution)/shard_map/ppermute | solution.py:411

commit v5 on v4

--- a/solution.py
+++ b/solution.py
@@ -269,8 +269,8 @@
 
 
 def total(values):
-    part = jnp.sum(spread(values, ("z", "x")), axis=0)
-    return spread(repeated(part, ("grp", "core")), ("grp", "core"))
+    part = jnp.sum(spread(values, ("grp", "x", "core")), axis=0)
+    return spread(repeated(part, "z"), "z")
 
 
 def least_squares(columns, beta):
@@ -433,7 +433,7 @@
         else:
             sums = call(
                 gram_kernel,
-                shape(chips, 1, LANES),
+                shape(groups * xs * 2, 1, LANES),
                 [smem(), smem()] + [vmem()] * 7,
                 400_000,
                 500_000,

time: 177 us -> 175 us (0.989)
  no operation moved by 1% of the time
where the time goes in v5:
time: 175 us; the launch traced here: 174 us
  blocking collectives  104 us (59%)
  starting transfers between devices  40.4 us (23%)
  Pallas kernels  17.2 us (10%)
  local copies, waits for them, and re-layouts  6.62 us (4%)
  waiting for transfers between devices  6.15 us (4%)
    all_to_all x4, blocking collectives, spread(): return lax.all_to_all(value, axis, 0, 0)  77.9 us
    all_to_all x1, starting transfers between devices, spread(): return lax.all_to_all(value, axis, 0, 0)  22.8 us
    all_gather x3, blocking collectives, per_device(): pieces = lax.all_gather(pieces, 'core')  14.5 us
    ppermute x3, starting transfers between devices, per_device(): other = lax.ppermute(send_across, SUB, across)  13.8 us
    unnamed x22, local copies, waits for them, and re-layouts  6.51 us
    all_to_all x1, waiting for transfers between devices, spread(): return lax.all_to_all(value, axis, 0, 0)  6.13 us
    all_gather x3, blocking collectives, per_device(): pair = lax.all_gather(rims, 'core')  5.67 us
    all_gather x3, blocking collectives, per_device(): shared = (core, margin, base, lax.all_gather(carried, 'core'), other, pair)  5.56 us
  transfers between devices with their start and end apart: 7, of which 1 were waited for; matrix products, arithmetic and copies ran while one was open for 0% of the time, Pallas kernels for 4%

profile of v5, /device:TPU:1, one launch (start us, length us, event | category | flops | bytes accessed | tf_op | source)
XLA Modules:
  0.0 174.3 jit_solution(9190452165485685735)
XLA Ops:
  0.0 2.1 %shard_map.73 = f32[64,4,128]{2,1,0:T(4,128)} custom-call(s32[1]{0:T(128)} %bitcast.core_ref, f32[8,2048]{1,0:T(8,128)} %bitcast.31, f32[48,2048]{1,0:T(8,128)} %bitcast.25), custom_call_target="tpu_custom_call" | custom-call | flops 3000000 | bytes 1500000 | tf_op jit(solution)/shard_map/pallas_call | solution.py:365
  2.1 22.8 %all-to-all-start = ((f32[64,4,128]{2,1,0:T(4,128)}), f32[64,4,128]{2,1,0:T(4,128)S(1)}, u32[]{:S(2)}, u32[]{:S(2)}) async-start(f32[64,4,128]{2,1,0:T(4,128)} %shard_map.73), calls=%async_computation | async-start | bytes 262144 | tf_op jit(solution)/shard_map/all_to_all | solution.py:264
  24.9 1.9 %copy-done.3 = f32[1,1,32,3,64,64]{5,4,3,2,1,0:T(8,128)S(1)} copy-done((f32[1,1,32,3,64,64]{5,4,3,2,1,0:T(8,128)S(1)}, f32[1,1,32,3,64,64]{5,4,3,2,1,0:T(8,128)}, u32[]{:S(2)}) %copy-start.3) | copy-done | bytes 1572888
  28.5 2.2 %shard_map.74 = (bf16[2048,128]{1,0:T(8,128)(2,1)S(1)}, bf16[48,4096]{1,0:T(8,128)(2,1)S(1)}, f32[1,2048]{1,0:T(1,128)S(1)}, bf16[32,256,128]{2,1,0:T(8,128)(2,1)S(1)}) custom-call(f32[48,2048]{1,0:T(8,128)S(1)} %bitcast.26, f32[1,2048]{1,0:T(1,128)S(1)} %bitcast.46, f32[32,3,64,64]{3,2,1,0:T(8,128)S(1)} %bitcast.24), custom_call_target="tpu_custom_call" | custom-call | flops 2000000 | bytes 6000000 | tf_op jit(solution)/shard_map/pallas_call | solution.py:378
  30.7 1.3 copy-done
  32.1 1.6 shard_map.75.coarse_ref
  33.7 6.1 %all-to-all-done = f32[64,4,128]{2,1,0:T(4,128)S(1)} async-done(((f32[64,4,128]{2,1,0:T(4,128)}), f32[64,4,128]{2,1,0:T(4,128)S(1)}, u32[]{:S(2)}, u32[]{:S(2)}) %all-to-all-start) | async-done | bytes 131104 | tf_op jit(solution)/shard_map/all_to_all | solution.py:264
  39.8 5.4 %all-gather = f32[128,4,128]{2,1,0:T(4,128)S(1)} all-gather(f32[64,4,128]{2,1,0:T(4,128)S(1)} %all-to-all-done), channel_id=2, replica_groups=mesh['grp'=8,'z'=16,'x'=4,'core'=2] {'core'}, dimensions={0}, use_global_device_ids=true | all-gather | bytes 393216 | tf_op jit(solution)/shard_map/all_gather | solution.py:401
  45.2 1.3 shard_map.76
  46.5 1.9 %all-gather.1 = f32[6,8,512]{2,1,0:T(8,128)S(1)} all-gather(f32[3,8,512]{2,1,0:T(8,128)S(1)} %get-tuple-element.30), channel_id=3, replica_groups=mesh['grp'=8,'z'=16,'x'=4,'core'=2] {'core'}, dimensions={0}, use_global_device_ids=true | all-gather | bytes 147456 | tf_op jit(solution)/shard_map/all_gather | solution.py:412
  48.4 1.3 collective-permute-start
  49.7 4.5 %collective-permute-start.1 = (f32[8,512]{1,0:T(8,128)S(1)}, f32[8,512]{1,0:T(8,128)S(1)}, u32[]{:S(2)}, u32[]{:S(2)}) collective-permute-start(f32[8,512]{1,0:T(8,128)S(1)} %get-tuple-element.31), channel_id=1, source_target_pairs={{1,2},{2,1},{3,4},{4,3},{5,6},{6,5},{7,8},{8,7},{9,10},{10,9},{11,... | collective-permute-start | bytes 49160 | tf_op jit(solution)/shard_map/ppermute | solution.py:411
  54.3 1.6 copy-done.1
  55.9 1.3 shard_map.77.base_ref
  57.2 1.9 %all-gather.2 = f32[4,8,512]{2,1,0:T(8,128)S(1)} all-gather(f32[2,8,512]{2,1,0:T(8,128)S(1)} %collective-permute-done), channel_id=4, replica_groups=mesh['grp'=8,'z'=16,'x'=4,'core'=2] {'core'}, dimensions={0}, use_global_device_ids=true | all-gather | bytes 98304 | tf_op jit(solution)/shard_map/all_gather | solution.py:423
  60.0 22.7 %all_to_all.25 = f32[64,4,128]{2,1,0:T(4,128)S(1)} all-to-all(f32[64,4,128]{2,1,0:T(4,128)S(1)} %get-tuple-element.33), channel_id=1, replica_groups=mesh['grp'=8,'z'=16,'x'=4,'core'=2] {'z','x'}, dimensions={0} | all-to-all | bytes 262144 | tf_op jit(solution)/shard_map/all_to_all | solution.py:264
  82.6 4.6 %all-gather.3 = f32[128,4,128]{2,1,0:T(4,128)S(1)} all-gather(f32[64,4,128]{2,1,0:T(4,128)S(1)} %all_to_all.25), channel_id=5, replica_groups=mesh['grp'=8,'z'=16,'x'=4,'core'=2] {'core'}, dimensions={0}, use_global_device_ids=true | all-gather | bytes 393216 | tf_op jit(solution)/shard_map/all_gather | solution.py:401
  87.2 1.3 shard_map.79
  88.5 1.9 %all-gather.4 = f32[6,8,512]{2,1,0:T(8,128)S(1)} all-gather(f32[3,8,512]{2,1,0:T(8,128)S(1)} %get-tuple-element.36), channel_id=6, replica_groups=mesh['grp'=8,'z'=16,'x'=4,'core'=2] {'core'}, dimensions={0}, use_global_device_ids=true | all-gather | bytes 147456 | tf_op jit(solution)/shard_map/all_gather | solution.py:412
  90.4 1.3 collective-permute-start.2
  91.7 4.7 %collective-permute-start.3 = (f32[8,512]{1,0:T(8,128)S(1)}, f32[8,512]{1,0:T(8,128)S(1)}, u32[]{:S(2)}, u32[]{:S(2)}) collective-permute-start(f32[8,512]{1,0:T(8,128)S(1)} %get-tuple-element.37), channel_id=1, source_target_pairs={{1,2},{2,1},{3,4},{4,3},{5,6},{6,5},{7,8},{8,7},{9,10},{10,9},{11,... | collective-permute-start | bytes 49160 | tf_op jit(solution)/shard_map/ppermute | solution.py:411
  96.4 1.3 shard_map.80.base_ref
  97.8 1.9 %all-gather.5 = f32[4,8,512]{2,1,0:T(8,128)S(1)} all-gather(f32[2,8,512]{2,1,0:T(8,128)S(1)} %collective-permute-done.2), channel_id=7, replica_groups=mesh['grp'=8,'z'=16,'x'=4,'core'=2] {'core'}, dimensions={0}, use_global_device_ids=true | all-gather | bytes 98304 | tf_op jit(solution)/shard_map/all_gather | solution.py:423
  100.5 22.6 %all_to_all.26 = f32[64,4,128]{2,1,0:T(4,128)S(1)} all-to-all(f32[64,4,128]{2,1,0:T(4,128)S(1)} %get-tuple-element.38), channel_id=1, replica_groups=mesh['grp'=8,'z'=16,'x'=4,'core'=2] {'z','x'}, dimensions={0} | all-to-all | bytes 262144 | tf_op jit(solution)/shard_map/all_to_all | solution.py:264
  123.2 4.6 %all-gather.6 = f32[128,4,128]{2,1,0:T(4,128)S(1)} all-gather(f32[64,4,128]{2,1,0:T(4,128)S(1)} %all_to_all.26), channel_id=8, replica_groups=mesh['grp'=8,'z'=16,'x'=4,'core'=2] {'core'}, dimensions={0}, use_global_device_ids=true | all-gather | bytes 393216 | tf_op jit(solution)/shard_map/all_gather | solution.py:401
  127.8 1.3 shard_map.82
  129.1 1.9 %all-gather.7 = f32[6,8,512]{2,1,0:T(8,128)S(1)} all-gather(f32[3,8,512]{2,1,0:T(8,128)S(1)} %get-tuple-element.41), channel_id=9, replica_groups=mesh['grp'=8,'z'=16,'x'=4,'core'=2] {'core'}, dimensions={0}, use_global_device_ids=true | all-gather | bytes 147456 | tf_op jit(solution)/shard_map/all_gather | solution.py:412
  132.2 4.6 %collective-permute-start.5 = (f32[8,512]{1,0:T(8,128)S(1)}, f32[8,512]{1,0:T(8,128)S(1)}, u32[]{:S(2)}, u32[]{:S(2)}) collective-permute-start(f32[8,512]{1,0:T(8,128)S(1)} %get-tuple-element.42), channel_id=1, source_target_pairs={{1,2},{2,1},{3,4},{4,3},{5,6},{6,5},{7,8},{8,7},{9,10},{10,9},{11,... | collective-permute-start | bytes 49160 | tf_op jit(solution)/shard_map/ppermute | solution.py:411
  136.9 1.3 shard_map.83.base_ref
  138.2 1.9 %all-gather.8 = f32[4,8,512]{2,1,0:T(8,128)S(1)} all-gather(f32[2,8,512]{2,1,0:T(8,128)S(1)} %collective-permute-done.4), channel_id=10, replica_groups=mesh['grp'=8,'z'=16,'x'=4,'core'=2] {'core'}, dimensions={0}, use_global_device_ids=true | all-gather | bytes 98304 | tf_op jit(solution)/shard_map/all_gather | solution.py:423
  140.9 17.7 %all_to_all.27 = f32[64,1,128]{2,1,0:T(1,128)S(1)} all-to-all(f32[64,1,128]{2,1,0:T(1,128)S(1)} %shard_map.84), channel_id=1, replica_groups=mesh['grp'=8,'z'=16,'x'=4,'core'=2] {'grp','x','core'}, dimensions={0} | all-to-all | bytes 65536 | tf_op jit(solution)/shard_map/all_to_all | solution.py:264
  158.7 14.8 %all_to_all.28.sums_ref = f32[16,1,128]{2,1,0:T(1,128)S(1)} all-to-all(f32[16,1,128]{2,1,0:T(1,128)S(1)} %broadcast_in_dim.4), channel_id=1, replica_groups=mesh['grp'=8,'z'=16,'x'=4,'core'=2] {'z'}, dimensions={0} | all-to-all | bytes 16384 | tf_op jit(solution)/shard_map/all_to_all | solution.py:264
  (36 shorter events, 6.6 us)
Async XLA Ops:
  2.1 37.7 %all-to-all-start = ((f32[64,4,128]{2,1,0:T(4,128)}), f32[64,4,128]{2,1,0:T(4,128)S(1)}, u32[]{:S(2)}, u32[]{:S(2)}) async-start(f32[64,4,128]{2,1,0:T(4,128)} %shard_map.73), calls=%async_computation | async-start | bytes 262144 | tf_op jit(solution)/shard_map/all_to_all | solution.py:264
  24.9 1.9 %copy-start.3 = (f32[1,1,32,3,64,64]{5,4,3,2,1,0:T(8,128)S(1)}, f32[1,1,32,3,64,64]{5,4,3,2,1,0:T(8,128)}, u32[]{:S(2)}) copy-start(f32[1,1,32,3,64,64]{5,4,3,2,1,0:T(8,128)} %param.9) | copy-start | bytes 4718596
  26.8 1.0 copy-start.4
  27.8 0.7 copy-start.7
  28.5 3.6 %copy-start.5 = (f32[1,48,6144]{2,1,0:T(8,128)S(1)}, f32[1,48,6144]{2,1,0:T(8,128)}, u32[]{:S(2)}) copy-start(f32[1,48,6144]{2,1,0:T(8,128)} %param.13) | copy-start | bytes 3538948
  30.7 1.3 copy-start
  32.1 13.1 %copy-start.6 = (f32[1,1,8,2048]{3,2,1,0:T(8,128)S(1)}, f32[1,1,8,2048]{3,2,1,0:T(8,128)}, u32[]{:S(2)}) copy-start(f32[1,1,8,2048]{3,2,1,0:T(8,128)} %param.7) | copy-start | bytes 196612
  32.1 13.1 %copy-start.9 = (s32[1,1,4,4]{3,2,1,0:T(4,128)S(1)}, s32[1,1,4,4]{3,2,1,0:T(4,128)}, u32[]{:S(2)}) copy-start(s32[1,1,4,4]{3,2,1,0:T(4,128)} %param.11) | copy-start | bytes 196
  33.6 16.0 %copy-start.10 = (s32[1,1,32,3]{2,1,3,0:T(1,128)S(1)}, s32[1,1,32,3]{2,1,3,0:T(1,128)}, u32[]{:S(2)}) copy-start(s32[1,1,32,3]{2,1,3,0:T(1,128)} %param.10) | copy-start | bytes 1156
  33.7 20.6 %copy-start.8 = (f32[1,1,2048]{2,1,0:T(1,128)S(1)}, f32[1,1,2048]{2,1,0:T(1,128)}, u32[]{:S(2)}) copy-start(f32[1,1,2048]{2,1,0:T(1,128)} %param.8) | copy-start | bytes 24580
  48.4 8.9 %collective-permute-start = (f32[2,8,512]{2,1,0:T(8,128)S(1)}, f32[2,8,512]{2,1,0:T(8,128)S(1)}, u32[]{:S(2)}, u32[]{:S(2)}) collective-permute-start(f32[2,8,512]{2,1,0:T(8,128)S(1)} %dynamic-slice_bitcast_fusion.2), channel_id=1, source_target_pairs={{0,128},{128,256},{256,384},{384,512},{512,640},{640,768},{768,896... | collective-permute-start | bytes 98312 | tf_op jit(solution)/shard_map/ppermute | solution.py:414
  49.7 9.3 %collective-permute-start.1 = (f32[8,512]{1,0:T(8,128)S(1)}, f32[8,512]{1,0:T(8,128)S(1)}, u32[]{:S(2)}, u32[]{:S(2)}) collective-permute-start(f32[8,512]{1,0:T(8,128)S(1)} %get-tuple-element.31), channel_id=1, source_target_pairs={{1,2},{2,1},{3,4},{4,3},{5,6},{6,5},{7,8},{8,7},{9,10},{10,9},{11,... | collective-permute-start | bytes 49160 | tf_op jit(solution)/shard_map/ppermute | solution.py:411
  54.3 1.6 copy-start.1
  59.1 37.3 %copy-start.2 = (bf16[32,256,128]{2,1,0:T(8,128)(2,1)S(1)}, bf16[32,256,128]{2,1,0:T(8,128)(2,1)}, u32[]{:S(2)}) copy-start(bf16[32,256,128]{2,1,0:T(8,128)(2,1)} %copy-done) | copy-start | bytes 6291460
  90.4 7.3 %collective-permute-start.2 = (f32[2,8,512]{2,1,0:T(8,128)S(1)}, f32[2,8,512]{2,1,0:T(8,128)S(1)}, u32[]{:S(2)}, u32[]{:S(2)}) collective-permute-start(f32[2,8,512]{2,1,0:T(8,128)S(1)} %dynamic-slice_bitcast_fusion.1), channel_id=1, source_target_pairs={{0,128},{128,256},{256,384},{384,512},{512,640},{640,768},{768,896... | collective-permute-start | bytes 98312 | tf_op jit(solution)/shard_map/ppermute | solution.py:414
  91.7 7.9 %collective-permute-start.3 = (f32[8,512]{1,0:T(8,128)S(1)}, f32[8,512]{1,0:T(8,128)S(1)}, u32[]{:S(2)}, u32[]{:S(2)}) collective-permute-start(f32[8,512]{1,0:T(8,128)S(1)} %get-tuple-element.37), channel_id=1, source_target_pairs={{1,2},{2,1},{3,4},{4,3},{5,6},{6,5},{7,8},{8,7},{9,10},{10,9},{11,... | collective-permute-start | bytes 49160 | tf_op jit(solution)/shard_map/ppermute | solution.py:411
  130.9 7.3 %collective-permute-start.4 = (f32[2,8,512]{2,1,0:T(8,128)S(1)}, f32[2,8,512]{2,1,0:T(8,128)S(1)}, u32[]{:S(2)}, u32[]{:S(2)}) collective-permute-start(f32[2,8,512]{2,1,0:T(8,128)S(1)} %dynamic-slice_bitcast_fusion), channel_id=1, source_target_pairs={{0,128},{128,256},{256,384},{384,512},{512,640},{640,768},{768,896... | collective-permute-start | bytes 98312 | tf_op jit(solution)/shard_map/ppermute | solution.py:414
  132.2 7.9 %collective-permute-start.5 = (f32[8,512]{1,0:T(8,128)S(1)}, f32[8,512]{1,0:T(8,128)S(1)}, u32[]{:S(2)}, u32[]{:S(2)}) collective-permute-start(f32[8,512]{1,0:T(8,128)S(1)} %get-tuple-element.42), channel_id=1, source_target_pairs={{1,2},{2,1},{3,4},{4,3},{5,6},{6,5},{7,8},{8,7},{9,10},{10,9},{11,... | collective-permute-start | bytes 49160 | tf_op jit(solution)/shard_map/ppermute | solution.py:411
